TPU v7x, 512 devices: a whole 4x4x16 slice. The times are simulated.
512 devices in a mesh: rowa: 16 (over z), rowb: 32 (over y, x, core).
Axes of the slice: x: 4, y: 4, z: 16, core: 2. Of those that a mesh axis runs over, the one named last changes fastest.
Arguments:
- slab: bfloat16 [262144, 1024], P(('rowa', 'rowb')), may hold values from -6 to 6, as said below
- panel: bfloat16 [64, 262144], P(None, ('rowa', 'rowb')), may hold values from -6 to 6
Outputs:
- basis_out: float32 [64, 262144], P(None, ('rowa', 'rowb'))
- factor_out: float32 [64, 64], replicated
Inputs may be any that keep to these rules, and one draw needn't show every extreme that they name: Real valued entries of the slab.
All inputs are finite; a program needn't handle non-finite values.
Results may differ from a plain program's by a relative error of at most 0.0055.
Values may be sent and summed in bfloat16 or wider, within the bound.
A program may use at most 64 MiB of HBM per device.

v0:
```python
import math

import jax
import jax.numpy as jnp
from jax import lax
from jax.sharding import PartitionSpec as P

ITERS = 3


def body(slab, panel):
    devices_a = lax.axis_size("rowa")
    devices_b = lax.axis_size("rowb")
    rows_total = panel.shape[1] * devices_a * devices_b
    current = panel
    basis = None
    lower = None
    for step in range(ITERS):
        partial_sum = jnp.dot(current, slab, preferred_element_type=jnp.float32)
        projected = lax.psum(partial_sum, ("rowa", "rowb"))
        projected_b = projected.astype(jnp.bfloat16)
        image = lax.dot_general(
            projected_b, slab, (((1,), (1,)), ((), ())), preferred_element_type=jnp.float32
        )
        local_gram = jnp.dot(image, image.T, precision=lax.Precision.HIGHEST)
        gram = lax.psum(local_gram, ("rowa", "rowb"))
        lower = jnp.linalg.cholesky(gram)
        basis = lax.linalg.triangular_solve(lower, image, left_side=True, lower=True)
        current = basis.astype(jnp.bfloat16)
    scale = math.sqrt(rows_total)
    return (basis * scale, lower.T / scale)


def solution(mesh):
    in_specs = (P(("rowa", "rowb"), None), P(None, ("rowa", "rowb")))
    out_specs = (P(None, ("rowa", "rowb")), P())
    return jax.shard_map(body, mesh=mesh, in_specs=in_specs, out_specs=out_specs, check_vma=False)
```

profile of v0, /device:TPU:1, one launch (start us, length us, event | category | flops | bytes accessed | tf_op | source)
XLA Modules:
  0.0 656.8 jit_solution(12679565002859070007)
XLA Ops:
  0.6 1.2 copy-done
  1.9 1.1 fusion.19
  3.0 112.2 %all-reduce.3 = bf16[64,1024]{1,0:T(8,128)(2,1)S(1)} all-reduce(f32[64,1024]{1,0:T(8,128)S(1)} %fusion.19), channel_id=1, replica_groups=mesh['rowa'=16,'rowb'=32] {'rowa','rowb'}, use_global_device_ids=true, to_apply=%region_0.0 | all-reduce | flops 65536 | bytes 393216 | tf_op jit(solution)/shard_map/psum | solution.py:20
  115.2 0.4 fusion.27
  115.6 0.3 fusion.20
  115.9 98.7 %psum.43 = f32[64,64]{0,1:T(8,128)S(1)} all-reduce(f32[64,64]{0,1:T(8,128)S(1)} %fusion.20), channel_id=1, replica_groups=mesh['rowa'=16,'rowb'=32] {'rowa','rowb'}, use_global_device_ids=true, to_apply=%region_1.0 | all-reduce | flops 4096 | bytes 32768 | tf_op jit(solution)/shard_map/psum | solution.py:26
  214.7 5.8 cholesky.59
  220.6 0.6 compare_reduce_fusion.2
  221.2 0.7 fusion.6
  221.9 4.9 custom-call.7
  226.8 0.3 convolution_convert_fusion.1
  227.1 0.3 fusion.21
  227.4 100.8 %all-reduce.4 = bf16[64,1024]{1,0:T(8,128)(2,1)S(1)} all-reduce(f32[64,1024]{1,0:T(8,128)S(1)} %fusion.21), channel_id=1, replica_groups=mesh['rowa'=16,'rowb'=32] {'rowa','rowb'}, use_global_device_ids=true, to_apply=%region_4.7 | all-reduce | flops 65536 | bytes 393216 | tf_op jit(solution)/shard_map/psum | solution.py:20
  328.3 0.4 fusion.26
  328.7 0.3 fusion.22
  329.0 99.4 %psum.45 = f32[64,64]{0,1:T(8,128)S(1)} all-reduce(f32[64,64]{0,1:T(8,128)S(1)} %fusion.22), channel_id=1, replica_groups=mesh['rowa'=16,'rowb'=32] {'rowa','rowb'}, use_global_device_ids=true, to_apply=%region_5.8 | all-reduce | flops 4096 | bytes 32768 | tf_op jit(solution)/shard_map/psum | solution.py:26
  428.5 5.8 cholesky.70
  434.4 0.6 compare_reduce_fusion.1
  435.0 0.7 fusion.7
  435.7 4.9 custom-call.8
  440.6 0.3 convolution_convert_fusion
  440.9 0.3 fusion.23
  441.3 101.3 %all-reduce.5 = bf16[64,1024]{1,0:T(8,128)(2,1)S(1)} all-reduce(f32[64,1024]{1,0:T(8,128)S(1)} %fusion.23), channel_id=1, replica_groups=mesh['rowa'=16,'rowb'=32] {'rowa','rowb'}, use_global_device_ids=true, to_apply=%region_6.9 | all-reduce | flops 65536 | bytes 393216 | tf_op jit(solution)/shard_map/psum | solution.py:20
  542.6 0.4 fusion.25
  543.0 0.3 fusion.24
  543.3 99.7 %psum.47 = f32[64,64]{0,1:T(8,128)S(1)} all-reduce(f32[64,64]{0,1:T(8,128)S(1)} %fusion.24), channel_id=1, replica_groups=mesh['rowa'=16,'rowb'=32] {'rowa','rowb'}, use_global_device_ids=true, to_apply=%region_7.10 | all-reduce | flops 4096 | bytes 32768 | tf_op jit(solution)/shard_map/psum | solution.py:26
  643.1 5.8 cholesky.81
  649.0 0.6 compare_reduce_fusion
  649.6 0.7 multiply_bitcast_fusion
  650.3 0.7 copy.10
  651.0 4.9 custom-call.9
  655.9 1.0 convolution_multiply_fusion
  (10 shorter events, 0.3 us)
Async XLA Ops:
  0.6 1.2 copy-start
where the time goes:
time: 658 us; the launch traced here: 657 us
  blocking collectives  612 us (93%)
  other arithmetic  36.2 us (6%)
    psum x3, blocking collectives, body(): projected = lax.psum(partial_sum, ('rowa', 'rowb'))  314 us
    psum x3, blocking collectives, body(): gram = lax.psum(local_gram, ('rowa', 'rowb'))  298 us
    another operation x9, other arithmetic, body(): lower = jnp.linalg.cholesky(gram)  19.6 us
    another operation x5, other arithmetic, body(): lax.linalg.triangular_solve(lower, image, left_side=True, lower=True)  16 us

commit v1 on v0

v1 whole, which is shorter than its diff:
```python
import functools
import math

import jax
import jax.numpy as jnp
from jax import lax
from jax.experimental import pallas as pl
from jax.experimental.pallas import tpu as pltpu
from jax.sharding import PartitionSpec as P

ITERS = 3
MESH = pl.DeviceIdType.MESH
F32 = jnp.float32
BF16 = jnp.bfloat16
LANE = 128
CORES = 2
PANEL = 4


def dot(a, b):
    return jnp.dot(a, b, preferred_element_type=F32)


def dot_t(a, b):
    return lax.dot_general(a, b, (((1,), (1,)), ((), ())), preferred_element_type=F32)


def split(v):
    high = v.astype(BF16)
    return high, (v - high.astype(F32)).astype(BF16)


def factor_rows(m, k):
    groups = [m[8 * i : 8 * i + 8, :] for i in range(k // 8)]
    full = groups[0].shape
    done = [[None] * 8 for _ in groups]
    for first in range(0, k, PANEL):
        g, s = divmod(first, 8)
        size = range(PANEL)
        rows = [jnp.broadcast_to(groups[g][s + q : s + q + 1, :], full) for q in size]
        cols = [
            {i: jnp.broadcast_to(groups[i][:, first + q : first + q + 1], full) for i in range(g, len(groups))}
            for q in size
        ]
        piv = [[jnp.broadcast_to(cols[r][g][s + q : s + q + 1, :], full) for r in size] for q in size]
        inv = []
        for q in size:
            inv.append(1.0 / piv[q][q])
            for r in range(q + 1, PANEL):
                t = piv[q][r] * inv[q]
                rows[r] = rows[r] - t * rows[q]
                for i in cols[r]:
                    cols[r][i] = cols[r][i] - t * cols[q][i]
                for w in range(r, PANEL):
                    piv[r][w] = piv[r][w] - t * piv[q][w]
            done[g][s + q] = rows[q] * lax.rsqrt(piv[q][q])
        for i in range(g, len(groups)):
            new = groups[i]
            for q in size:
                new = new - (cols[q][i] * inv[q]) * rows[q]
            groups[i] = new
    sub = lax.broadcasted_iota(jnp.int32, full, 0)
    out = []
    for rows in done:
        v = rows[0]
        for q in range(1, 8):
            v = jnp.where(sub == q, rows[q], v)
        out.append(v)
    return jnp.concatenate(out, axis=0)


def kernel(dims, tiles, scale, slab_ref, panel_ref, basis_ref, factor_ref,
           part, got_c, acc, got_1, mid, got_2, own, got_z, total, g_high, g_low, w_high, w_low, p_pad, sems):
    nz, ny, nx = dims
    k, d = panel_ref.shape[0], slab_ref.shape[1]
    nb = d // LANE
    half = part.shape[0] // CORES
    stream = half // 2
    rows_1 = (stream // nx, stream // ny)
    rows_2 = stream // (nx * ny)
    tile = 2 * rows_2 // tiles

    z = lax.axis_index("rowa")
    b = lax.axis_index("rowb")
    c = lax.rem(b, CORES)
    x = lax.rem(b // CORES, nx)
    y = b // (CORES * nx)

    def device(zz, yy, xx, cc):
        return (zz, (yy * nx + xx) * CORES + cc)

    other = device(z, y, x, 1 - c)
    peers_x = [device(z, y, lax.rem(x + q, nx), c) for q in range(1, nx)]
    peers_y = [device(z, lax.rem(y + q, ny), x, c) for q in range(1, ny)]
    peers_z = [device(lax.rem(z + q, nz), y, x, c) for q in range(1, nz)]

    barrier = pltpu.get_barrier_semaphore()
    everyone = [other] + peers_x + peers_y + peers_z
    for peer in everyone:
        pl.semaphore_signal(barrier, inc=1, device_id=peer, device_id_type=MESH)

    used = [0]

    def new_sems(n):
        at = used[0]
        used[0] += n
        return at

    def copy(src, dst, send, recv, peer):
        return pltpu.make_async_remote_copy(
            src_ref=src, dst_ref=dst, send_sem=sems.at[send], recv_sem=sems.at[recv], device_id=peer, device_id_type=MESH
        )

    at = 0
    for i in range(nb):
        left = slab_ref[:, i * LANE : (i + 1) * LANE].T
        g = dot(left, slab_ref[:, i * LANE :])
        for j in range(i, nb):
            part[at * LANE : (at + 1) * LANE, :] = g[:, (j - i) * LANE : (j - i + 1) * LANE]
            at += 1
    first = dot(panel_ref[...], slab_ref[...])
    for j in range(nb):
        part[at * LANE + j * k : at * LANE + (j + 1) * k, :] = first[:, j * LANE : (j + 1) * LANE]

    pl.semaphore_wait(barrier, len(everyone))

    sent = []
    s, r = new_sems(1), new_sems(1)
    cp = copy(part.at[pl.ds(pl.multiple_of((1 - c) * half, half), half)], got_c, s, r, other)
    cp.start()
    cp.wait_recv()
    sent.append(cp)
    acc[...] = part[pl.ds(pl.multiple_of(c * half, half), half), :] + got_c[...]

    streams = ((nx, x, peers_x, ny, y, peers_y), (ny, y, peers_y, nx, x, peers_x))
    waits = []
    for i, (n1, me1, peers1, _, _, _) in enumerate(streams):
        s, r = new_sems(n1 - 1), new_sems(n1 - 1)
        for q in range(1, n1):
            to = lax.rem(me1 + q, n1)
            src = acc.at[pl.ds(pl.multiple_of(i * stream + to * rows_1[i], 16), rows_1[i])]
            cp = copy(src, got_1.at[i, q - 1], s + q - 1, r + q - 1, peers1[q - 1])
            cp.start()
            waits.append(cp)
    for i, (n1, me1, _, _, _, _) in enumerate(streams):
        for cp in waits[i * (n1 - 1) : (i + 1) * (n1 - 1)]:
            cp.wait_recv()
        v = acc[pl.ds(pl.multiple_of(i * stream + me1 * rows_1[i], 16), rows_1[i]), :]
        for q in range(n1 - 1):
            v = v + got_1[i, q]
        mid[i] = v
    sent += waits

    waits = []
    for i, (_, _, _, n2, me2, peers2) in enumerate(streams):
        s, r = new_sems(n2 - 1), new_sems(n2 - 1)
        for q in range(1, n2):
            to = lax.rem(me2 + q, n2)
            src = mid.at[i, pl.ds(pl.multiple_of(to * rows_2, 16), rows_2)]
            cp = copy(src, got_2.at[i, q - 1], s + q - 1, r + q - 1, peers2[q - 1])
            cp.start()
            waits.append(cp)
    for i, (_, _, _, n2, me2, _) in enumerate(streams):
        for cp in waits[i * (n2 - 1) : (i + 1) * (n2 - 1)]:
            cp.wait_recv()
        v = mid[i, pl.ds(pl.multiple_of(me2 * rows_2, 16), rows_2), :]
        for q in range(n2 - 1):
            v = v + got_2[i, q]
        own[i * rows_2 : (i + 1) * rows_2, :] = v
    sent += waits

    owners = [(t * nz) // tiles for t in range(tiles)]
    bases = [c * half + x * rows_1[0] + y * rows_2, c * half + stream + y * rows_1[1] + x * rows_2]
    mine = (z * tiles + nz - 1) // nz
    is_owner = (mine * nz) // tiles == z
    half_tiles = tiles // 2
    s_z, r_z = new_sems(tiles), new_sems(nz - 1)

    def to_owner(t):
        slot = lax.rem(z - owners[t] + nz - 1 + nz, nz)
        return copy(own.at[pl.ds(t * tile, tile)], got_z.at[slot], s_z + t, r_z + slot, device(owners[t], y, x, c))

    for t in range(tiles):
        @pl.when(z != owners[t])
        def _():
            to_owner(t).start()

    def tile_rows(t, hi_half):
        base = jnp.where(hi_half, bases[1] + (t - half_tiles) * tile, bases[0] + t * tile)
        return pl.ds(pl.multiple_of(base, 16), tile)

    s_g, r_g = new_sems(nz - 1), new_sems(tiles)

    @pl.when(is_owner)
    def _():
        v = own[pl.ds(pl.multiple_of(mine * tile, 16), tile), :]
        for q in range(nz - 1):
            copy(own.at[pl.ds(0, tile)], got_z.at[q], s_z, r_z + q, other).wait_recv()
        for q in range(nz - 1):
            v = v + got_z[q]
        where = tile_rows(mine, mine >= half_tiles)
        total[where, :] = v
        for q in range(nz - 1):
            copy(total.at[where], total.at[where], s_g + q, r_g + mine, peers_z[q]).start()

    for t in range(tiles):
        i = t // half_tiles
        where = pl.ds(pl.multiple_of(bases[i] + (t - i * half_tiles) * tile, 16), tile)

        @pl.when(z != owners[t])
        def _():
            copy(total.at[where], total.at[where], s_g, r_g + t, other).wait_recv()

    waits = []
    for i, (_, _, _, n2, me2, peers2) in enumerate(streams):
        s, r = new_sems(n2 - 1), new_sems(n2 - 1)
        where = total.at[pl.ds(pl.multiple_of(bases[i], 16), rows_2)]
        for q in range(1, n2):
            cp = copy(where, where, s + q - 1, r + q - 1, peers2[q - 1])
            cp.start()
            waits.append(cp)
    for cp in waits:
        cp.wait_recv()
    sent += waits

    waits = []
    for i, (n1, me1, peers1, _, _, _) in enumerate(streams):
        s, r = new_sems(n1 - 1), new_sems(n1 - 1)
        where = total.at[pl.ds(pl.multiple_of(c * half + i * stream + me1 * rows_1[i], 16), rows_1[i])]
        for q in range(1, n1):
            cp = copy(where, where, s + q - 1, r + q - 1, peers1[q - 1])
            cp.start()
            waits.append(cp)
    for cp in waits:
        cp.wait_recv()
    sent += waits

    s, r = new_sems(1), new_sems(1)
    where = total.at[pl.ds(pl.multiple_of(c * half, half), half)]
    cp = copy(where, where, s, r, other)
    cp.start()
    cp.wait_recv()
    sent.append(cp)

    for cp in sent:
        cp.wait_send()
    for t in range(tiles):
        @pl.when(z != owners[t])
        def _():
            to_owner(t).wait_send()

    @pl.when(is_owner)
    def _():
        where = tile_rows(mine, mine >= half_tiles)
        for q in range(nz - 1):
            copy(total.at[where], total.at[where], s_g + q, r_g + mine, peers_z[q]).wait_send()

    at = 0
    for i in range(nb):
        for j in range(i, nb):
            v = total[at * LANE : (at + 1) * LANE, :]
            at += 1
            high, low = split(v)
            g_high[i * LANE : (i + 1) * LANE, j * LANE : (j + 1) * LANE] = high
            g_low[i * LANE : (i + 1) * LANE, j * LANE : (j + 1) * LANE] = low
            if j > i:
                high, low = split(v.T)
                g_high[j * LANE : (j + 1) * LANE, i * LANE : (i + 1) * LANE] = high
                g_low[j * LANE : (j + 1) * LANE, i * LANE : (i + 1) * LANE] = low

    w_high[0:k, :] = jnp.zeros((k, d), BF16)
    w_low[0:k, :] = jnp.zeros((k, d), BF16)
    p_pad[k : 2 * k, :] = jnp.zeros((k, d), BF16)
    current = jnp.concatenate(
        [total[at * LANE + j * k : at * LANE + (j + 1) * k, :] for j in range(nb)], axis=1
    )
    row = lax.broadcasted_iota(jnp.int32, (k, 2 * k), 0)
    col = lax.broadcasted_iota(jnp.int32, (k, 2 * k), 1)
    eye = jnp.where(col == row + k, 1.0, 0.0)
    for step in range(ITERS):
        pb = current.astype(BF16)
        p_pad[0:k, :] = pb
        wh, wl = split(dot(pb, g_high[...]) + dot(pb, g_low[...]))
        m = factor_rows(dot_t(wh, p_pad[...]) + dot_t(wl, p_pad[...]) + eye, k)
        mh, ml = split(m)
        if step < ITERS - 1:
            w_high[k : 2 * k, :] = wh
            w_low[k : 2 * k, :] = wl
            current = dot(mh, w_high[...]) + (dot(mh, w_low[...]) + dot(ml, w_high[...]))
        else:
            rows = slab_ref.shape[0]
            ih, il = split(dot_t(pb, slab_ref[...]))
            w_high[k : 2 * k, 0:rows] = ih
            w_low[k : 2 * k, 0:rows] = il
            ih, il = w_high[:, 0:rows], w_low[:, 0:rows]
            basis_ref[...] = (dot(mh, ih) + (dot(mh, il) + dot(ml, ih))) * scale
            factor_ref[...] = jnp.where(col >= row, m, 0.0)[:, 0:k] * (1.0 / scale)


def body(sizes, slab, panel):
    nz, ny, nx, tiles = sizes
    rows, d = slab.shape
    k = panel.shape[0]
    nb = d // LANE
    blocks = nb * (nb + 1) // 2 + nb * k // LANE
    half = blocks * LANE // CORES
    stream = half // 2
    rows_1, rows_2 = stream // nx, stream // (nx * ny)
    tile = 2 * rows_2 // tiles
    scale = math.sqrt(rows * nz * ny * nx * CORES)
    n_sems = 4 + 4 * (nx - 1 + ny - 1) * 2 + 2 * (tiles + nz - 1)
    return pl.pallas_call(
        functools.partial(kernel, (nz, ny, nx), tiles, scale),
        out_shape=(jax.ShapeDtypeStruct((k, rows), F32), jax.ShapeDtypeStruct((k, k), F32)),
        in_specs=[pl.BlockSpec(memory_space=pltpu.VMEM)] * 2,
        out_specs=(pl.BlockSpec(memory_space=pltpu.VMEM),) * 2,
        scratch_shapes=[
            pltpu.VMEM((2 * half, LANE), F32),
            pltpu.VMEM((half, LANE), F32),
            pltpu.VMEM((half, LANE), F32),
            pltpu.VMEM((2, nx - 1, rows_1, LANE), F32),
            pltpu.VMEM((2, rows_1, LANE), F32),
            pltpu.VMEM((2, ny - 1, rows_2, LANE), F32),
            pltpu.VMEM((2 * rows_2, LANE), F32),
            pltpu.VMEM((nz - 1, tile, LANE), F32),
            pltpu.VMEM((2 * half, LANE), F32),
            pltpu.VMEM((d, d), BF16),
            pltpu.VMEM((d, d), BF16),
            pltpu.VMEM((2 * k, d), BF16),
            pltpu.VMEM((2 * k, d), BF16),
            pltpu.VMEM((2 * k, d), BF16),
            pltpu.SemaphoreType.DMA((n_sems,)),
        ],
        compiler_params=pltpu.CompilerParams(
            collective_id=0, has_side_effects=True, vmem_limit_bytes=40 * 1024 * 1024
        ),
        cost_estimate=pl.CostEstimate(flops=3 * 10**9, bytes_accessed=3 * 10**6, transcendentals=0),
    )(slab, panel)


def solution(mesh):
    nz = mesh.shape["rowa"]
    side = math.isqrt(mesh.shape["rowb"] // CORES)
    tiles = 10 if nz == 16 else 2
    in_specs = (P(("rowa", "rowb"), None), P(None, ("rowa", "rowb")))
    out_specs = (P(None, ("rowa", "rowb")), P())
    return jax.shard_map(
        functools.partial(body, (nz, side, side, tiles)),
        mesh=mesh, in_specs=in_specs, out_specs=out_specs, check_vma=False,
    )
```

time: 658 us -> 84.4 us (0.13)
  blocking collectives: 612 us -> 0 us
  Pallas kernels: 0 us -> 80.3 us
  other arithmetic: 36.2 us -> 0 us
    psum x6 -> x0, blocking collectives: 612 us -> none  [the longest x3 314 us: body(): projected = lax.psum(partial_sum, ('rowa', 'rowb'))]
    pallas_call x0 -> x1, Pallas kernels: none -> 80.3 us  [body(): pl.pallas_call(functools.partial(kernel, (nz, ny, nx), tiles, scale), out...]
    another operation x14 -> x0, other arithmetic: 35.6 us -> none  [the longest x9 19.6 us: body(): lower = jnp.linalg.cholesky(gram)]
where the time goes in v1:
time: 84.4 us; the launch traced here: 84.2 us
  Pallas kernels  80.3 us (95%)
  local copies, waits for them, and re-layouts  3.33 us (4%)
    pallas_call x1, Pallas kernels, body(): pl.pallas_call(functools.partial(kernel, (nz, ny, nx), tiles, scale), out...  80.3 us
    unnamed x6, local copies, waits for them, and re-layouts  3.33 us

profile of v1, /device:TPU:1, one launch (start us, length us, event | category | flops | bytes accessed | tf_op | source)
XLA Modules:
  0.0 84.2 jit_solution(5514072479647261016)
XLA Ops:
  0.6 0.0 copy-start
  0.6 1.2 %copy-done = bf16[512,1024]{1,0:T(8,128)(2,1)S(1)} copy-done((bf16[512,1024]{1,0:T(8,128)(2,1)S(1)}, bf16[512,1024]{1,0:T(8,128)(2,1)}, u32[]{:S(2)}) %copy-start) | copy-done | bytes 1048600
  1.9 0.0 copy-start.1
  1.9 0.8 copy-done.1
  2.7 80.3 %shard_map.41 = (f32[64,512]{1,0:T(8,128)S(1)}, f32[64,64]{1,0:T(8,128)S(1)}) custom-call(bf16[512,1024]{1,0:T(8,128)(2,1)S(1)} %copy-done, bf16[64,512]{1,0:T(8,128)(2,1)S(1)} %copy-done.1), custom_call_target="tpu_custom_call" | custom-call | flops 3000000000 | bytes 3000000 | tf_op jit(solution)/shard_map/pallas_call | solution.py:312
  83.0 0.7 copy.6
  83.6 0.6 copy.7
Async XLA Ops:
  0.6 1.2 %copy-start = (bf16[512,1024]{1,0:T(8,128)(2,1)S(1)}, bf16[512,1024]{1,0:T(8,128)(2,1)}, u32[]{:S(2)}) copy-start(bf16[512,1024]{1,0:T(8,128)(2,1)} %slab_ref.1) | copy-start | bytes 3145732
  1.9 0.8 copy-start.1

commit v2 on v1

--- a/solution.py
+++ b/solution.py
@@ -69,8 +69,8 @@
     return jnp.concatenate(out, axis=0)
 
 
-def kernel(dims, tiles, scale, slab_ref, panel_ref, basis_ref, factor_ref,
-           part, got_c, acc, got_1, mid, got_2, own, got_z, total, g_high, g_low, w_high, w_low, p_pad, sems):
+def reduce_kernel(dims, tiles, slab_ref, panel_ref, total,
+                  part, got_c, acc, got_1, mid, got_2, own, got_z, sems):
     nz, ny, nx = dims
     k, d = panel_ref.shape[0], slab_ref.shape[1]
     nb = d // LANE
@@ -254,6 +254,11 @@
         where = tile_rows(mine, mine >= half_tiles)
         for q in range(nz - 1):
             copy(total.at[where], total.at[where], s_g + q, r_g + mine, peers_z[q]).wait_send()
+
+
+def passes_kernel(scale, slab_ref, total, basis_ref, factor_ref, g_high, g_low, w_high, w_low, p_pad):
+    k, d = p_pad.shape[0] // 2, slab_ref.shape[1]
+    nb = d // LANE
 
     at = 0
     for i in range(nb):
@@ -309,11 +314,13 @@
     tile = 2 * rows_2 // tiles
     scale = math.sqrt(rows * nz * ny * nx * CORES)
     n_sems = 4 + 4 * (nx - 1 + ny - 1) * 2 + 2 * (tiles + nz - 1)
-    return pl.pallas_call(
-        functools.partial(kernel, (nz, ny, nx), tiles, scale),
-        out_shape=(jax.ShapeDtypeStruct((k, rows), F32), jax.ShapeDtypeStruct((k, k), F32)),
-        in_specs=[pl.BlockSpec(memory_space=pltpu.VMEM)] * 2,
-        out_specs=(pl.BlockSpec(memory_space=pltpu.VMEM),) * 2,
+    params = functools.partial(pltpu.CompilerParams, vmem_limit_bytes=40 * 1024 * 1024)
+    vmem = pl.BlockSpec(memory_space=pltpu.VMEM)
+    total = pl.pallas_call(
+        functools.partial(reduce_kernel, (nz, ny, nx), tiles),
+        out_shape=jax.ShapeDtypeStruct((2 * half, LANE), F32),
+        in_specs=[vmem] * 2,
+        out_specs=vmem,
         scratch_shapes=[
             pltpu.VMEM((2 * half, LANE), F32),
             pltpu.VMEM((half, LANE), F32),
@@ -323,19 +330,26 @@
             pltpu.VMEM((2, ny - 1, rows_2, LANE), F32),
             pltpu.VMEM((2 * rows_2, LANE), F32),
             pltpu.VMEM((nz - 1, tile, LANE), F32),
-            pltpu.VMEM((2 * half, LANE), F32),
+            pltpu.SemaphoreType.DMA((n_sems,)),
+        ],
+        compiler_params=params(collective_id=0, has_side_effects=True),
+        cost_estimate=pl.CostEstimate(flops=10**9, bytes_accessed=10**7, transcendentals=0),
+    )(slab, panel)
+    return pl.pallas_call(
+        functools.partial(passes_kernel, scale),
+        out_shape=(jax.ShapeDtypeStruct((k, rows), F32), jax.ShapeDtypeStruct((k, k), F32)),
+        in_specs=[vmem] * 2,
+        out_specs=(vmem,) * 2,
+        scratch_shapes=[
             pltpu.VMEM((d, d), BF16),
             pltpu.VMEM((d, d), BF16),
             pltpu.VMEM((2 * k, d), BF16),
             pltpu.VMEM((2 * k, d), BF16),
             pltpu.VMEM((2 * k, d), BF16),
-            pltpu.SemaphoreType.DMA((n_sems,)),
         ],
-        compiler_params=pltpu.CompilerParams(
-            collective_id=0, has_side_effects=True, vmem_limit_bytes=40 * 1024 * 1024
-        ),
-        cost_estimate=pl.CostEstimate(flops=3 * 10**9, bytes_accessed=3 * 10**6, transcendentals=0),
-    )(slab, panel)
+        compiler_params=params(),
+        cost_estimate=pl.CostEstimate(flops=2 * 10**9, bytes_accessed=3 * 10**6, transcendentals=0),
+    )(slab, total)
 
 
 def solution(mesh):

time: 84.4 us -> 83.8 us (level)
  local copies, waits for them, and re-layouts: 3.33 us -> 2.06 us
    unnamed x6 -> x4, local copies, waits for them, and re-layouts: 3.33 us -> 2.06 us
    pallas_call x1 -> x2, Pallas kernels: 80.3 us -> 80.9 us  [the longest x1 68 us: body(): pl.pallas_call(functools.partial(reduce_kernel, (nz, ny, nx), tiles), out...]
where the time goes in v2:
time: 83.8 us; the launch traced here: 83.6 us
  Pallas kernels  80.9 us (97%)
  local copies, waits for them, and re-layouts  2.06 us (2%)
    pallas_call x1, Pallas kernels, body(): pl.pallas_call(functools.partial(reduce_kernel, (nz, ny, nx), tiles), out...  68 us
    pallas_call x1, Pallas kernels, body(): pl.pallas_call(functools.partial(passes_kernel, scale), out_shape=(jax.Sh...  12.9 us
    unnamed x4, local copies, waits for them, and re-layouts  2.06 us

profile of v2, /device:TPU:1, one launch (start us, length us, event | category | flops | bytes accessed | tf_op | source)
XLA Modules:
  0.0 83.6 jit_solution(7824835148481563672)
XLA Ops:
  0.6 0.0 copy-start
  0.6 1.2 %copy-done = bf16[512,1024]{1,0:T(8,128)(2,1)S(1)} copy-done((bf16[512,1024]{1,0:T(8,128)(2,1)S(1)}, bf16[512,1024]{1,0:T(8,128)(2,1)}, u32[]{:S(2)}) %copy-start) | copy-done | bytes 1048600
  1.9 0.0 copy-start.1
  1.9 0.8 %copy-done.1 = bf16[64,512]{1,0:T(8,128)(2,1)S(1)} copy-done((bf16[64,512]{1,0:T(8,128)(2,1)S(1)}, bf16[64,512]{1,0:T(8,128)(2,1)}, u32[]{:S(2)}) %copy-start.1) | copy-done | bytes 65560
  2.7 68.0 %shard_map.41.total = f32[5120,128]{1,0:T(8,128)S(1)} custom-call(bf16[512,1024]{1,0:T(8,128)(2,1)S(1)} %copy-done, bf16[64,512]{1,0:T(8,128)(2,1)S(1)} %copy-done.1), custom_call_target="tpu_custom_call" | custom-call | flops 1000000000 | bytes 10000000 | tf_op jit(solution)/shard_map/pallas_call | solution.py:319
  70.7 12.9 %shard_map.42 = (f32[64,512]{1,0:T(8,128)}, f32[64,64]{1,0:T(8,128)}) custom-call(bf16[512,1024]{1,0:T(8,128)(2,1)S(1)} %copy-done, f32[5120,128]{1,0:T(8,128)S(1)} %shard_map.41.total), custom_call_target="tpu_custom_call" | custom-call | flops 2000000000 | bytes 3000000 | tf_op jit(solution)/shard_map/pallas_call | solution.py:338
Async XLA Ops:
  0.6 1.2 %copy-start = (bf16[512,1024]{1,0:T(8,128)(2,1)S(1)}, bf16[512,1024]{1,0:T(8,128)(2,1)}, u32[]{:S(2)}) copy-start(bf16[512,1024]{1,0:T(8,128)(2,1)} %slab_ref.3) | copy-start | bytes 3145732
  1.9 0.8 %copy-start.1 = (bf16[64,512]{1,0:T(8,128)(2,1)S(1)}, bf16[64,512]{1,0:T(8,128)(2,1)}, u32[]{:S(2)}) copy-start(bf16[64,512]{1,0:T(8,128)(2,1)} %panel_ref.1) | copy-start | bytes 196612

commit v3 on v0

v3 whole, which is shorter than its diff:
```python
import functools
import math

import jax
import jax.numpy as jnp
from jax import lax
from jax.experimental import pallas as pl
from jax.experimental.pallas import tpu as pltpu
from jax.sharding import PartitionSpec as P

ITERS = 3
MESH = pl.DeviceIdType.MESH
F32 = jnp.float32
BF16 = jnp.bfloat16
LANE = 128
CORES = 2
PANEL = 4


def dot(a, b):
    return jnp.dot(a, b, preferred_element_type=F32)


def dot_t(a, b):
    return lax.dot_general(a, b, (((1,), (1,)), ((), ())), preferred_element_type=F32)


def split(v):
    high = v.astype(BF16)
    return high, (v - high.astype(F32)).astype(BF16)


def factor_rows(m, k):
    groups = [m[8 * i : 8 * i + 8, :] for i in range(k // 8)]
    full = groups[0].shape
    done = [[None] * 8 for _ in groups]
    for first in range(0, k, PANEL):
        g, s = divmod(first, 8)
        size = range(PANEL)
        rows = [jnp.broadcast_to(groups[g][s + q : s + q + 1, :], full) for q in size]
        cols = [
            {i: jnp.broadcast_to(groups[i][:, first + q : first + q + 1], full) for i in range(g, len(groups))}
            for q in size
        ]
        piv = [[jnp.broadcast_to(cols[r][g][s + q : s + q + 1, :], full) for r in size] for q in size]
        inv = []
        for q in size:
            inv.append(1.0 / piv[q][q])
            for r in range(q + 1, PANEL):
                t = piv[q][r] * inv[q]
                rows[r] = rows[r] - t * rows[q]
                for i in cols[r]:
                    cols[r][i] = cols[r][i] - t * cols[q][i]
                for w in range(r, PANEL):
                    piv[r][w] = piv[r][w] - t * piv[q][w]
            done[g][s + q] = rows[q] * lax.rsqrt(piv[q][q])
        for i in range(g, len(groups)):
            new = groups[i]
            for q in size:
                new = new - (cols[q][i] * inv[q]) * rows[q]
            groups[i] = new
    sub = lax.broadcasted_iota(jnp.int32, full, 0)
    out = []
    for rows in done:
        v = rows[0]
        for q in range(1, 8):
            v = jnp.where(sub == q, rows[q], v)
        out.append(v)
    return jnp.concatenate(out, axis=0)


JOBS = (
    (
        (("g", 0, 0, 8), ("g", 3, 3, 8), ("g", 4, 4, 8), ("g", 7, 7, 8), ("p", 0, 4)),
        (("g", 1, 1, 8), ("g", 2, 2, 8), ("g", 5, 5, 8), ("g", 6, 6, 8), ("p", 4, 8)),
    ),
)
CHUNKS = len(JOBS)
Z_GROUP = 8
ROWS = (20 * LANE,)


def places(ch, cc, k):
    at, out = 0, []
    for job in JOBS[ch][cc]:
        for j in range(job[-2], job[-1]):
            out.append((job[0], job[1] if job[0] == "g" else 0, j, at))
            at += LANE if job[0] == "g" else k
    return out


def z_tiles(ch):
    mine = ROWS[ch] // 32
    tile = 8 if mine <= 8 * Z_GROUP else 16
    return mine // tile, tile


def flip(bit, mask):
    return bit + mask - 2 * bit * mask


def reduce_kernel(dims, slab, panel, g_high, g_low, first, slab_2, panel_2, *refs):
    part, got_1, got_2, own, got_z, own_t, total = (refs[i * CHUNKS : (i + 1) * CHUNKS] for i in range(7))
    (sems,) = refs[7 * CHUNKS :]
    slabs, panels = (slab, slab_2), (panel, panel_2)
    nz, ny, nx = dims
    k = panel.shape[0]

    z = lax.axis_index("rowa")
    b = lax.axis_index("rowb")
    c = lax.rem(b, CORES)
    x = lax.rem(b // CORES, nx)
    y = b // (CORES * nx)

    def device(zz, yy, xx, cc):
        return (zz, (yy * nx + xx) * CORES + cc)

    def ring_pairs(i, n):
        low = lax.rem(i, 2)
        return (lax.rem((i + 1) // 2, 2), i + 1 - 2 * low), (i // 2, n - 1 - i)

    pair_x, pair_y = ring_pairs(x, nx), ring_pairs(y, ny)
    z_bit, z_at = lax.rem(z, 2), z // 2
    pair_z = (z_bit, z + 1 - 2 * z_bit), (z_bit, lax.rem(z - 1 + 2 * z_bit + nz, nz))

    def cube(which, mask):
        return device(
            pair_z[which][1] if mask & 4 else z,
            pair_y[which][1] if mask & 2 else y,
            pair_x[which][1] if mask & 1 else x,
            c,
        )

    def index(which, mask, size):
        at = flip(pair_x[which][0], mask & 1) + 2 * flip(pair_y[which][0], mask // 2 & 1)
        return at + 4 * flip(pair_z[which][0], mask // 4) if size == 8 else at

    other = device(z, y, x, 1 - c)
    peers_z = [device(2 * lax.rem(z_at + q, Z_GROUP) + z_bit, y, x, c) for q in range(1, Z_GROUP)]

    barrier = pltpu.get_barrier_semaphore()
    everyone = [other] + [cube(s, m) for s in range(2) for m in range(1, 8)] + peers_z
    for peer in everyone:
        pl.semaphore_signal(barrier, inc=1, device_id=peer, device_id_type=MESH)

    used = [0]

    def new_sems(count):
        used[0] += count
        return used[0] - count

    def copy(src, dst, send, recv, peer):
        return pltpu.make_async_remote_copy(
            src_ref=src, dst_ref=dst, send_sem=sems.at[send], recv_sem=sems.at[recv], device_id=peer, device_id_type=MESH
        )

    sent = []
    pl.semaphore_wait(barrier, len(everyone))

    at = new_sems(4)
    exchange = [
        copy(slab, slab_2, at, at + 1, other),
        copy(panel, panel_2, at + 2, at + 3, other),
    ]
    for cp in exchange:
        cp.start()
    sent += exchange

    def work(ch, which):
        for cc in range(CORES):
            @pl.when(c == cc)
            def _():
                at = 0
                for job in JOBS[ch][cc]:
                    j0, j1 = job[-2:]
                    if job[0] == "g":
                        left, step = slabs[which][:, job[1] * LANE : (job[1] + 1) * LANE].T, LANE
                    else:
                        left, step = panels[which][...], k
                    v = dot(left, slabs[which][:, j0 * LANE : j1 * LANE])
                    for j in range(j1 - j0):
                        new = v[:, j * LANE : (j + 1) * LANE]
                        if which:
                            new = part[ch][at : at + step, :] + new
                        part[ch][at : at + step, :] = new
                        at += step

    def steps(ch):
        size = ROWS[ch] // 2
        piece, last = size // 8, size // 32
        tiles, tile = z_tiles(ch)
        owners = [((t * Z_GROUP) // tiles + ch) % Z_GROUP for t in range(tiles)]
        spot = lax.rem(z_at - ch + Z_GROUP, Z_GROUP)
        mine = (spot * tiles + Z_GROUP - 1) // Z_GROUP
        is_owner = (mine * Z_GROUP) // tiles == spot
        started = {}

        def rows(off, count):
            return pl.ds(off if isinstance(off, int) else pl.multiple_of(off, 8), count)

        off_1 = [s * size + index(s, 0, 8) * piece for s in range(2)]
        off_2 = [off_1[s] + index(1 - s, 0, 4) * last for s in range(2)]

        def start(key, src, dst, peer):
            at = new_sems(2)
            cp = started[key] = copy(src, dst, at, at + 1, peer)
            cp.start()
            sent.append(cp)

        def begin():
            for s in range(2):
                for m in range(1, 8):
                    src = part[ch].at[rows(s * size + index(s, m, 8) * piece, piece)]
                    start(("r1", s, m), src, got_1[ch].at[s, m - 1], cube(s, m))

        def second():
            for s in range(2):
                v = part[ch][rows(off_1[s], piece), :]
                for m in range(1, 8):
                    started["r1", s, m].wait_recv()
                    v = v + got_1[ch][s, m - 1]
                part[ch][rows(off_1[s], piece), :] = v
                for m in range(1, 4):
                    src = part[ch].at[rows(off_1[s] + index(1 - s, m, 4) * last, last)]
                    start(("r2", s, m), src, got_2[ch].at[s, m - 1], cube(1 - s, m))

        s_z, r_z, s_g, r_g = new_sems(tiles), new_sems(Z_GROUP - 1), new_sems(Z_GROUP - 1), new_sems(tiles)

        def to_owner(t):
            slot = lax.rem(z_at - owners[t] + 2 * Z_GROUP - 1, Z_GROUP)
            src = own[ch].at[pl.ds(t * tile, tile)]
            return copy(src, got_z[ch].at[slot], s_z + t, r_z + slot, device(2 * owners[t] + z_bit, y, x, c))

        def to_all(q):
            where = own_t[ch].at[rows(mine * tile, tile)]
            return copy(where, where, s_g + q, r_g + mine, peers_z[q])

        def to_z():
            for s in range(2):
                v = part[ch][rows(off_2[s], last), :]
                for m in range(1, 4):
                    started["r2", s, m].wait_recv()
                    v = v + got_2[ch][s, m - 1]
                own[ch][s * last : (s + 1) * last, :] = v
            for t in range(tiles):
                @pl.when(z_at != owners[t])
                def _():
                    to_owner(t).start()

        def at_owner():
            @pl.when(is_owner)
            def _():
                v = own[ch][rows(mine * tile, tile), :]
                for q in range(Z_GROUP - 1):
                    copy(own[ch].at[pl.ds(0, tile)], got_z[ch].at[q], s_z, r_z + q, other).wait_recv()
                    v = v + got_z[ch][q]
                own_t[ch][rows(mine * tile, tile), :] = v
                for q in range(Z_GROUP - 1):
                    to_all(q).start()

        def from_z():
            for t in range(tiles):
                where = own_t[ch].at[pl.ds(t * tile, tile)]

                @pl.when(z_at != owners[t])
                def _():
                    copy(where, where, s_g, r_g + t, other).wait_recv()
            for s in range(2):
                where = rows(off_2[s], last)
                for m in range(1, 4):
                    start(("g2", s, m), own_t[ch].at[pl.ds(s * last, last)], total[ch].at[c, where], cube(1 - s, m))
                total[ch][c, where, :] = own_t[ch][s * last : (s + 1) * last, :]

        def gather():
            for s in range(2):
                for m in range(1, 4):
                    started["g2", s, m].wait_recv()
                where = total[ch].at[c, rows(off_1[s], piece)]
                for m in range(1, 8):
                    start(("g1", s, m), where, where, cube(s, m))

        def across():
            for s in range(2):
                for m in range(1, 8):
                    started["g1", s, m].wait_recv()
                where = total[ch].at[c, pl.ds(s * size, size)]
                start(("c", s), where, where, other)

        def finish():
            for s in range(2):
                started["c", s].wait_recv()
            for cc in range(CORES):
                for kind, i, j, at in places(ch, cc, k):
                    if kind == "p":
                        first[:, j * LANE : (j + 1) * LANE] = total[ch][cc, at : at + k, :]
                        continue
                    v = total[ch][cc, at : at + LANE, :]
                    for a, e, w in ((i, j, v), (j, i, v.T))[: 2 if j > i else 1]:
                        high, low = split(w)
                        g_high[a * LANE : (a + 1) * LANE, e * LANE : (e + 1) * LANE] = high
                        g_low[a * LANE : (a + 1) * LANE, e * LANE : (e + 1) * LANE] = low

        def drain():
            for t in range(tiles):
                @pl.when(z_at != owners[t])
                def _():
                    to_owner(t).wait_send()

            @pl.when(is_owner)
            def _():
                for q in range(Z_GROUP - 1):
                    to_all(q).wait_send()

        return begin, (second, to_z, at_owner, from_z, gather, across, finish), drain

    chunks = [steps(ch) for ch in range(CHUNKS)]
    for ch in range(CHUNKS):
        work(ch, 0)
    for cp in exchange:
        cp.wait_recv()
    for ch in range(CHUNKS):
        work(ch, 1)
        chunks[ch][0]()
    for at in range(len(chunks[0][1])):
        for ch in range(CHUNKS):
            chunks[ch][1][at]()
    for cp in sent:
        cp.wait_send()
    for ch in range(CHUNKS):
        chunks[ch][2]()


def passes_kernel(scale, slab, g_high, g_low, first, basis_ref, factor_ref, w_high, w_low, p_pad):
    k, d = first.shape
    w_high[0:k, :] = jnp.zeros((k, d), BF16)
    w_low[0:k, :] = jnp.zeros((k, d), BF16)
    p_pad[k : 2 * k, :] = jnp.zeros((k, d), BF16)
    current = first[...]
    row = lax.broadcasted_iota(jnp.int32, (k, 2 * k), 0)
    col = lax.broadcasted_iota(jnp.int32, (k, 2 * k), 1)
    eye = jnp.where(col == row + k, 1.0, 0.0)
    for step in range(ITERS):
        pb = current.astype(BF16)
        p_pad[0:k, :] = pb
        wh, wl = split(dot(pb, g_high[...]) + dot(pb, g_low[...]))
        m = factor_rows(dot_t(wh, p_pad[...]) + dot_t(wl, p_pad[...]) + eye, k)
        mh, ml = split(m)
        if step < ITERS - 1:
            w_high[k : 2 * k, :] = wh
            w_low[k : 2 * k, :] = wl
            current = dot(mh, w_high[...]) + (dot(mh, w_low[...]) + dot(ml, w_high[...]))
        else:
            rows = slab.shape[0]
            ih, il = split(dot_t(pb, slab[...]))
            w_high[k : 2 * k, 0:rows] = ih
            w_low[k : 2 * k, 0:rows] = il
            ih, il = w_high[:, 0:rows], w_low[:, 0:rows]
            basis_ref[...] = (dot(mh, ih) + (dot(mh, il) + dot(ml, ih))) * scale
            factor_ref[...] = jnp.where(col >= row, m, 0.0)[:, 0:k] * (1.0 / scale)


def body(sizes, slab, panel):
    nz, ny, nx = sizes
    rows, d = slab.shape
    k = panel.shape[0]
    scale = math.sqrt(rows * nz * ny * nx * CORES)
    tiles = [z_tiles(ch) for ch in range(CHUNKS)]
    n_sems = 4 + sum(4 * (7 + 3) * 2 + 2 * (t + Z_GROUP - 1) + 4 for t, _ in tiles)
    params = functools.partial(pltpu.CompilerParams, vmem_limit_bytes=36 * 1024 * 1024)
    vmem = pl.BlockSpec(memory_space=pltpu.VMEM)

    def each(shape):
        return [pltpu.VMEM(shape(ch), F32) for ch in range(CHUNKS)]

    g_high, g_low, first = pl.pallas_call(
        functools.partial(reduce_kernel, (nz, ny, nx)),
        out_shape=(
            jax.ShapeDtypeStruct((d, d), BF16), jax.ShapeDtypeStruct((d, d), BF16), jax.ShapeDtypeStruct((k, d), F32)
        ),
        in_specs=[vmem] * 2,
        out_specs=(vmem,) * 3,
        scratch_shapes=[
            pltpu.VMEM((rows, d), BF16),
            pltpu.VMEM((k, rows), BF16),
            *each(lambda ch: (ROWS[ch], LANE)),
            *each(lambda ch: (2, 7, ROWS[ch] // 16, LANE)),
            *each(lambda ch: (2, 3, ROWS[ch] // 64, LANE)),
            *each(lambda ch: (ROWS[ch] // 32, LANE)),
            *each(lambda ch: (Z_GROUP - 1, tiles[ch][1], LANE)),
            *each(lambda ch: (ROWS[ch] // 32, LANE)),
            *each(lambda ch: (CORES, ROWS[ch], LANE)),
            pltpu.SemaphoreType.DMA((n_sems,)),
        ],
        compiler_params=params(collective_id=0, has_side_effects=True),
        cost_estimate=pl.CostEstimate(flops=10**9, bytes_accessed=10**7, transcendentals=0),
    )(slab, panel)
    return pl.pallas_call(
        functools.partial(passes_kernel, scale),
        out_shape=(jax.ShapeDtypeStruct((k, rows), F32), jax.ShapeDtypeStruct((k, k), F32)),
        in_specs=[vmem] * 4,
        out_specs=(vmem,) * 2,
        scratch_shapes=[
            pltpu.VMEM((2 * k, d), BF16),
            pltpu.VMEM((2 * k, d), BF16),
            pltpu.VMEM((2 * k, d), BF16),
        ],
        compiler_params=params(),
        cost_estimate=pl.CostEstimate(flops=2 * 10**9, bytes_accessed=3 * 10**6, transcendentals=0),
    )(slab, g_high, g_low, first)


def solution(mesh):
    nz = mesh.shape["rowa"]
    side = math.isqrt(mesh.shape["rowb"] // CORES)
    in_specs = (P(("rowa", "rowb"), None), P(None, ("rowa", "rowb")))
    out_specs = (P(None, ("rowa", "rowb")), P())
    return jax.shard_map(
        functools.partial(body, (nz, side, side)),
        mesh=mesh, in_specs=in_specs, out_specs=out_specs, check_vma=False,
    )
```

time: 658 us -> 83.1 us (0.13)
  blocking collectives: 612 us -> 0 us
  Pallas kernels: 0 us -> 80.1 us
  other arithmetic: 36.2 us -> 0 us
    psum x6 -> x0, blocking collectives: 612 us -> none  [the longest x3 314 us: body(): projected = lax.psum(partial_sum, ('rowa', 'rowb'))]
    pallas_call x0 -> x2, Pallas kernels: none -> 80.1 us  [the longest x1 67.8 us: body(): pl.pallas_call(functools.partial(reduce_kernel, (nz, ny, nx)), out_shape=...]
    another operation x14 -> x0, other arithmetic: 35.6 us -> none  [the longest x9 19.6 us: body(): lower = jnp.linalg.cholesky(gram)]
where the time goes in v3:
time: 83.1 us; the launch traced here: 82.9 us
  Pallas kernels  80.1 us (96%)
  local copies, waits for them, and re-layouts  2.06 us (2%)
    pallas_call x1, Pallas kernels, body(): pl.pallas_call(functools.partial(reduce_kernel, (nz, ny, nx)), out_shape=...  67.8 us
    pallas_call x1, Pallas kernels, body(): pl.pallas_call(functools.partial(passes_kernel, scale), out_shape=(jax.Sh...  12.4 us
    unnamed x4, local copies, waits for them, and re-layouts  2.06 us

profile of v3, /device:TPU:1, one launch (start us, length us, event | category | flops | bytes accessed | tf_op | source)
XLA Modules:
  0.0 82.9 jit_solution(6242866382734526759)
XLA Ops:
  0.6 0.0 copy-start
  0.6 1.2 %copy-done = bf16[512,1024]{1,0:T(8,128)(2,1)S(1)} copy-done((bf16[512,1024]{1,0:T(8,128)(2,1)S(1)}, bf16[512,1024]{1,0:T(8,128)(2,1)}, u32[]{:S(2)}) %copy-start) | copy-done | bytes 1048600
  1.9 0.0 copy-start.1
  1.9 0.8 %copy-done.1 = bf16[64,512]{1,0:T(8,128)(2,1)S(1)} copy-done((bf16[64,512]{1,0:T(8,128)(2,1)S(1)}, bf16[64,512]{1,0:T(8,128)(2,1)}, u32[]{:S(2)}) %copy-start.1) | copy-done | bytes 65560
  2.7 67.8 %shard_map.41 = (bf16[1024,1024]{1,0:T(8,128)(2,1)S(1)}, bf16[1024,1024]{1,0:T(8,128)(2,1)S(1)}, f32[64,1024]{1,0:T(8,128)S(1)}) custom-call(bf16[512,1024]{1,0:T(8,128)(2,1)S(1)} %copy-done, bf16[64,512]{1,0:T(8,128)(2,1)S(1)} %copy-done.1), custom_call_target="tpu_custom_call" | custom-call | flops 1000000000 | bytes 10000000 | tf_op jit(solution)/shard_map/pallas_call | solution.py:375
  70.5 12.4 %shard_map.42 = (f32[64,512]{1,0:T(8,128)}, f32[64,64]{1,0:T(8,128)}) custom-call(bf16[512,1024]{1,0:T(8,128)(2,1)S(1)} %copy-done, bf16[1024,1024]{1,0:T(8,128)(2,1)S(1)} %get-tuple-element.5.g_high, bf16[1024,1024]{1,0:T(8,128)(2,1)S(1)} %get-tuple-element.6.g_low, f32[64,1024]{1,0:T(8,128)S(1)} %get-tuple-element.7.first), custom_call_target="tpu_custom_call" | custom-call | flops 2000000000 | bytes 3000000 | tf_op jit(solution)/shard_map/pallas_call | solution.py:397
Async XLA Ops:
  0.6 1.2 %copy-start = (bf16[512,1024]{1,0:T(8,128)(2,1)S(1)}, bf16[512,1024]{1,0:T(8,128)(2,1)}, u32[]{:S(2)}) copy-start(bf16[512,1024]{1,0:T(8,128)(2,1)} %slab.3) | copy-start | bytes 3145732
  1.9 0.8 %copy-start.1 = (bf16[64,512]{1,0:T(8,128)(2,1)S(1)}, bf16[64,512]{1,0:T(8,128)(2,1)}, u32[]{:S(2)}) copy-start(bf16[64,512]{1,0:T(8,128)(2,1)} %panel.1) | copy-start | bytes 196612

commit v4 on v3

--- a/solution.py
+++ b/solution.py
@@ -14,7 +14,7 @@
 BF16 = jnp.bfloat16
 LANE = 128
 CORES = 2
-PANEL = 4
+PANEL = 8
 
 
 def dot(a, b):
@@ -45,7 +45,7 @@
         piv = [[jnp.broadcast_to(cols[r][g][s + q : s + q + 1, :], full) for r in size] for q in size]
         inv = []
         for q in size:
-            inv.append(1.0 / piv[q][q])
+            inv.append(pl.reciprocal(piv[q][q]))
             for r in range(q + 1, PANEL):
                 t = piv[q][r] * inv[q]
                 rows[r] = rows[r] - t * rows[q]
@@ -70,14 +70,12 @@
 
 
 JOBS = (
-    (
-        (("g", 0, 0, 8), ("g", 3, 3, 8), ("g", 4, 4, 8), ("g", 7, 7, 8), ("p", 0, 4)),
-        (("g", 1, 1, 8), ("g", 2, 2, 8), ("g", 5, 5, 8), ("g", 6, 6, 8), ("p", 4, 8)),
-    ),
+    ((("g", 0, 0, 8),), (("g", 2, 2, 8), ("g", 6, 6, 8))),
+    ((("g", 3, 3, 8), ("g", 4, 4, 8), ("g", 7, 7, 8), ("p", 0, 4)), (("g", 1, 1, 8), ("g", 5, 5, 8), ("p", 4, 8))),
 )
 CHUNKS = len(JOBS)
 Z_GROUP = 8
-ROWS = (20 * LANE,)
+ROWS = (8 * LANE, 12 * LANE)
 
 
 def places(ch, cc, k):
@@ -321,9 +319,11 @@
     for ch in range(CHUNKS):
         work(ch, 1)
         chunks[ch][0]()
-    for at in range(len(chunks[0][1])):
+    count = len(chunks[0][1])
+    for at in range(count + CHUNKS - 1):
         for ch in range(CHUNKS):
-            chunks[ch][1][at]()
+            if 0 <= at - ch < count:
+                chunks[ch][1][at - ch]()
     for cp in sent:
         cp.wait_send()
     for ch in range(CHUNKS):
@@ -343,6 +343,9 @@
         pb = current.astype(BF16)
         p_pad[0:k, :] = pb
         wh, wl = split(dot(pb, g_high[...]) + dot(pb, g_low[...]))
+        if step == ITERS - 1:
+            rows = slab.shape[0]
+            ih, il = split(dot_t(pb, slab[...]))
         m = factor_rows(dot_t(wh, p_pad[...]) + dot_t(wl, p_pad[...]) + eye, k)
         mh, ml = split(m)
         if step < ITERS - 1:
@@ -350,8 +353,6 @@
             w_low[k : 2 * k, :] = wl
             current = dot(mh, w_high[...]) + (dot(mh, w_low[...]) + dot(ml, w_high[...]))
         else:
-            rows = slab.shape[0]
-            ih, il = split(dot_t(pb, slab[...]))
             w_high[k : 2 * k, 0:rows] = ih
             w_low[k : 2 * k, 0:rows] = il
             ih, il = w_high[:, 0:rows], w_low[:, 0:rows]

time: 83.1 us -> 80.9 us (0.974)
  Pallas kernels: 80.1 us -> 78 us
    pallas_call x1, Pallas kernels: 12.4 us -> 10.2 us  [body(): pl.pallas_call(functools.partial(passes_kernel, scale), out_shape=(jax.Sh...]
where the time goes in v4:
time: 80.9 us; the launch traced here: 80.7 us
  Pallas kernels  78 us (96%)
  local copies, waits for them, and re-layouts  2.06 us (3%)
    pallas_call x1, Pallas kernels, body(): pl.pallas_call(functools.partial(reduce_kernel, (nz, ny, nx)), out_shape=...  67.9 us
    pallas_call x1, Pallas kernels, body(): pl.pallas_call(functools.partial(passes_kernel, scale), out_shape=(jax.Sh...  10.2 us
    unnamed x4, local copies, waits for them, and re-layouts  2.06 us

profile of v4, /device:TPU:1, one launch (start us, length us, event | category | flops | bytes accessed | tf_op | source)
XLA Modules:
  0.0 80.7 jit_solution(12135402552522278863)
XLA Ops:
  0.6 0.0 copy-start
  0.6 1.2 %copy-done = bf16[512,1024]{1,0:T(8,128)(2,1)S(1)} copy-done((bf16[512,1024]{1,0:T(8,128)(2,1)S(1)}, bf16[512,1024]{1,0:T(8,128)(2,1)}, u32[]{:S(2)}) %copy-start) | copy-done | bytes 1048600
  1.9 0.0 copy-start.1
  1.9 0.8 %copy-done.1 = bf16[64,512]{1,0:T(8,128)(2,1)S(1)} copy-done((bf16[64,512]{1,0:T(8,128)(2,1)S(1)}, bf16[64,512]{1,0:T(8,128)(2,1)}, u32[]{:S(2)}) %copy-start.1) | copy-done | bytes 65560
  2.7 67.9 %shard_map.41 = (bf16[1024,1024]{1,0:T(8,128)(2,1)S(1)}, bf16[1024,1024]{1,0:T(8,128)(2,1)S(1)}, f32[64,1024]{1,0:T(8,128)S(1)}) custom-call(bf16[512,1024]{1,0:T(8,128)(2,1)S(1)} %copy-done, bf16[64,512]{1,0:T(8,128)(2,1)S(1)} %copy-done.1), custom_call_target="tpu_custom_call" | custom-call | flops 1000000000 | bytes 10000000 | tf_op jit(solution)/shard_map/pallas_call | solution.py:376
  70.6 10.2 %shard_map.42 = (f32[64,512]{1,0:T(8,128)}, f32[64,64]{1,0:T(8,128)}) custom-call(bf16[512,1024]{1,0:T(8,128)(2,1)S(1)} %copy-done, bf16[1024,1024]{1,0:T(8,128)(2,1)S(1)} %get-tuple-element.5.g_high, bf16[1024,1024]{1,0:T(8,128)(2,1)S(1)} %get-tuple-element.6.g_low, f32[64,1024]{1,0:T(8,128)S(1)} %get-tuple-element.7.first), custom_call_target="tpu_custom_call" | custom-call | flops 2000000000 | bytes 3000000 | tf_op jit(solution)/shard_map/pallas_call | solution.py:398
Async XLA Ops:
  0.6 1.2 %copy-start = (bf16[512,1024]{1,0:T(8,128)(2,1)S(1)}, bf16[512,1024]{1,0:T(8,128)(2,1)}, u32[]{:S(2)}) copy-start(bf16[512,1024]{1,0:T(8,128)(2,1)} %slab.3) | copy-start | bytes 3145732
  1.9 0.8 %copy-start.1 = (bf16[64,512]{1,0:T(8,128)(2,1)S(1)}, bf16[64,512]{1,0:T(8,128)(2,1)}, u32[]{:S(2)}) copy-start(bf16[64,512]{1,0:T(8,128)(2,1)} %panel.1) | copy-start | bytes 196612

commit v5 on v0

v5 whole, which is shorter than its diff:
```python
import functools
import math

import jax
import jax.numpy as jnp
from jax import lax
from jax.experimental import pallas as pl
from jax.experimental.pallas import tpu as pltpu
from jax.sharding import PartitionSpec as P

ITERS = 3
MESH = pl.DeviceIdType.MESH
F32 = jnp.float32
BF16 = jnp.bfloat16
LANE = 128
CORES = 2
PANEL = 8


def dot(a, b):
    return jnp.dot(a, b, preferred_element_type=F32)


def dot_t(a, b):
    return lax.dot_general(a, b, (((1,), (1,)), ((), ())), preferred_element_type=F32)


def split(v):
    high = v.astype(BF16)
    return high, (v - high.astype(F32)).astype(BF16)


def factor_rows(m, k):
    groups = [m[8 * i : 8 * i + 8, :] for i in range(k // 8)]
    full = groups[0].shape
    done = [[None] * 8 for _ in groups]
    for first in range(0, k, PANEL):
        g, s = divmod(first, 8)
        size = range(PANEL)
        rows = [jnp.broadcast_to(groups[g][s + q : s + q + 1, :], full) for q in size]
        cols = [
            {i: jnp.broadcast_to(groups[i][:, first + q : first + q + 1], full) for i in range(g, len(groups))}
            for q in size
        ]
        piv = [[jnp.broadcast_to(cols[r][g][s + q : s + q + 1, :], full) for r in size] for q in size]
        inv = []
        for q in size:
            inv.append(pl.reciprocal(piv[q][q]))
            for r in range(q + 1, PANEL):
                t = piv[q][r] * inv[q]
                rows[r] = rows[r] - t * rows[q]
                for i in cols[r]:
                    cols[r][i] = cols[r][i] - t * cols[q][i]
                for w in range(r, PANEL):
                    piv[r][w] = piv[r][w] - t * piv[q][w]
            done[g][s + q] = rows[q] * lax.rsqrt(piv[q][q])
        for i in range(g, len(groups)):
            new = groups[i]
            for q in size:
                new = new - (cols[q][i] * inv[q]) * rows[q]
            groups[i] = new
    sub = lax.broadcasted_iota(jnp.int32, full, 0)
    out = []
    for rows in done:
        v = rows[0]
        for q in range(1, 8):
            v = jnp.where(sub == q, rows[q], v)
        out.append(v)
    return jnp.concatenate(out, axis=0)


JOBS = (
    (("g", 0, 0, 8), ("g", 3, 3, 8), ("g", 4, 4, 8), ("g", 7, 7, 8), ("p", 0, 4)),
    (("g", 1, 1, 8), ("g", 2, 2, 8), ("g", 5, 5, 8), ("g", 6, 6, 8), ("p", 4, 8)),
)
SIZES = (12 * LANE, 8 * LANE)
FIRST = (0, SIZES[0])
HALF = sum(SIZES)
PIECE = tuple(size // 8 for size in SIZES)
LAST = tuple(size // 64 for size in SIZES)
LAST_AT = (0, LAST[0])
OWN = sum(LAST)
FAR = 4


def places(cc, k):
    at, out = 0, []
    for job in JOBS[cc]:
        for j in range(job[-2], job[-1]):
            out.append((job[0], job[1] if job[0] == "g" else 0, j, at))
            at += LANE if job[0] == "g" else k
    return out


def flip(bit, mask):
    return bit + mask - 2 * bit * mask


def reduce_kernel(dims, slab, panel, g_high, g_low, first, part, got_c, got_1, got_2, own, got_z, own_t, total, sems):
    nz, ny, nx = dims
    k = panel.shape[0]

    z = lax.axis_index("rowa")
    b = lax.axis_index("rowb")
    c = lax.rem(b, CORES)
    x = lax.rem(b // CORES, nx)
    y = b // (CORES * nx)

    def device(zz, yy, xx, cc):
        return (zz, (yy * nx + xx) * CORES + cc)

    def ring_pairs(i, n):
        low = lax.rem(i, 2)
        return (lax.rem((i + 1) // 2, 2), i + 1 - 2 * low), (i // 2, n - 1 - i)

    def line_pairs(i, n):
        low = lax.rem(i, 2)
        return (low, i + 1 - 2 * low), (low, lax.rem(i - 1 + 2 * low + n, n))

    z_low, z_at = lax.rem(z, 2), z // 2
    pair_x, pair_y, pair_z = ring_pairs(x, nx), ring_pairs(y, ny), line_pairs(z, nz)
    pair_z2 = tuple((bit, 2 * at + z_low) for bit, at in line_pairs(z_at, nz // 2))

    def pick(pair, family):
        return tuple(a + family * (e - a) for a, e in zip(*pair))

    families = [lax.rem(s + c, 2) for s in range(2)]
    groups = [
        (
            [pick(pair, f) for pair in (pair_x, pair_y, pair_z)],
            [pick(pair_x, 1 - f), pick(pair_y, 1 - f), pick(pair_z2, f)],
        )
        for f in families
    ]

    def peer(s, step, mask):
        px, py, pz = groups[s][step]
        return device(pz[1] if mask & 4 else z, py[1] if mask & 2 else y, px[1] if mask & 1 else x, c)

    def index(s, step, mask):
        return sum(flip(bit, mask >> i & 1) * (1 << i) for i, (bit, _) in enumerate(groups[s][step]))

    other = device(z, y, x, 1 - c)
    far = [device(lax.rem(z + q * (nz // FAR), nz), y, x, c) for q in range(1, FAR)]

    barrier = pltpu.get_barrier_semaphore()
    everyone = far + [other] + [peer(s, 0, m) for s in range(2) for m in range(1, 8)]
    everyone += [peer(s, 1, m) for s in range(2) for m in range(4, 8)]
    for device_id in everyone:
        pl.semaphore_signal(barrier, inc=1, device_id=device_id, device_id_type=MESH)

    used, sent, started = [0], [], {}

    def start(key, src, dst, device_id):
        at = used[0]
        used[0] += 2
        cp = started[key] = pltpu.make_async_remote_copy(
            src_ref=src, dst_ref=dst, send_sem=sems.at[at], recv_sem=sems.at[at + 1],
            device_id=device_id, device_id_type=MESH,
        )
        cp.start()
        sent.append(cp)

    def rows(off, count):
        return pl.ds(off if isinstance(off, int) else pl.multiple_of(off, 8), count)

    for cc in range(CORES):
        at = 0
        for job in JOBS[cc]:
            j0, j1 = job[-2:]
            if job[0] == "g":
                left, step = slab[:, job[1] * LANE : (job[1] + 1) * LANE].T, LANE
            else:
                left, step = panel[...], k
            v = dot(left, slab[:, j0 * LANE : j1 * LANE])
            for j in range(j1 - j0):
                part[cc, at : at + step, :] = v[:, j * LANE : (j + 1) * LANE]
                at += step

    pl.semaphore_wait(barrier, len(everyone))

    streams = range(2)
    off_1 = [FIRST[s] + index(s, 0, 0) * PIECE[s] for s in streams]
    off_2 = [off_1[s] + index(s, 1, 0) * LAST[s] for s in streams]

    for s in streams:
        where = pl.ds(FIRST[s], SIZES[s])
        start(("c", s), part.at[1 - c, where], got_c.at[where], other)
    for s in streams:
        started["c", s].wait_recv()
        where = pl.ds(FIRST[s], SIZES[s])
        got_c[where, :] = part[c, where, :] + got_c[where, :]
        for m in range(1, 8):
            src = got_c.at[rows(FIRST[s] + index(s, 0, m) * PIECE[s], PIECE[s])]
            start((1, s, m), src, got_1.at[m - 1, pl.ds(FIRST[s] // 8, PIECE[s])], peer(s, 0, m))
    for s in streams:
        v = got_c[rows(off_1[s], PIECE[s]), :]
        for m in range(1, 8):
            started[1, s, m].wait_recv()
            v = v + got_1[m - 1, FIRST[s] // 8 : FIRST[s] // 8 + PIECE[s], :]
        got_c[rows(off_1[s], PIECE[s]), :] = v
        for m in range(1, 8):
            src = got_c.at[rows(off_1[s] + index(s, 1, m) * LAST[s], LAST[s])]
            start((2, s, m), src, got_2.at[m - 1, pl.ds(LAST_AT[s], LAST[s])], peer(s, 1, m))
    for s in streams:
        v = got_c[rows(off_2[s], LAST[s]), :]
        for m in range(1, 8):
            started[2, s, m].wait_recv()
            v = v + got_2[m - 1, LAST_AT[s] : LAST_AT[s] + LAST[s], :]
        own[LAST_AT[s] : LAST_AT[s] + LAST[s], :] = v

    me_far = z // (nz // FAR)
    send_z, recv_z = used[0], used[0] + FAR - 1
    used[0] += 2 * FAR - 1

    def far_copy(q, slot):
        return pltpu.make_async_remote_copy(
            src_ref=own, dst_ref=got_z.at[slot], send_sem=sems.at[send_z + q - 1], recv_sem=sems.at[recv_z + slot],
            device_id=far[q - 1], device_id_type=MESH,
        )

    for q in range(1, FAR):
        cp = far_copy(q, me_far)
        cp.start()
        sent.append(cp)
    got_z[me_far] = own[...]
    for q in range(1, FAR):
        far_copy(q, lax.rem(me_far + q, FAR)).wait_recv()
    v = got_z[0]
    for q in range(1, FAR):
        v = v + got_z[q]
    own_t[...] = v

    for s in streams:
        where = rows(off_2[s], LAST[s])
        for m in range(1, 8):
            start((3, s, m), own_t.at[pl.ds(LAST_AT[s], LAST[s])], total.at[c, where], peer(s, 1, m))
        total[c, where, :] = own_t[LAST_AT[s] : LAST_AT[s] + LAST[s], :]
    for s in streams:
        for m in range(1, 8):
            started[3, s, m].wait_recv()
        where = total.at[c, rows(off_1[s], PIECE[s])]
        for m in range(1, 8):
            start((4, s, m), where, where, peer(s, 0, m))
    for s in streams:
        for m in range(1, 8):
            started[4, s, m].wait_recv()
        where = total.at[c, pl.ds(FIRST[s], SIZES[s])]
        start((5, s), where, where, other)

    def whole(half):
        for cc in range(CORES):
            @pl.when(half == cc)
            def _():
                for kind, i, j, at in places(cc, k):
                    if kind == "p":
                        first[:, j * LANE : (j + 1) * LANE] = total[cc, at : at + k, :]
                        continue
                    v = total[cc, at : at + LANE, :]
                    for a, e, w in ((i, j, v), (j, i, v.T))[: 2 if j > i else 1]:
                        high, low = split(w)
                        g_high[a * LANE : (a + 1) * LANE, e * LANE : (e + 1) * LANE] = high
                        g_low[a * LANE : (a + 1) * LANE, e * LANE : (e + 1) * LANE] = low

    whole(c)
    for s in streams:
        started[5, s].wait_recv()
    whole(1 - c)
    for cp in sent:
        cp.wait_send()


def passes_kernel(scale, slab, g_high, g_low, first, basis_ref, factor_ref, w_high, w_low, p_pad):
    k, d = first.shape
    w_high[0:k, :] = jnp.zeros((k, d), BF16)
    w_low[0:k, :] = jnp.zeros((k, d), BF16)
    p_pad[k : 2 * k, :] = jnp.zeros((k, d), BF16)
    current = first[...]
    row = lax.broadcasted_iota(jnp.int32, (k, 2 * k), 0)
    col = lax.broadcasted_iota(jnp.int32, (k, 2 * k), 1)
    eye = jnp.where(col == row + k, 1.0, 0.0)
    for step in range(ITERS):
        pb = current.astype(BF16)
        p_pad[0:k, :] = pb
        wh, wl = split(dot(pb, g_high[...]) + dot(pb, g_low[...]))
        if step == ITERS - 1:
            rows = slab.shape[0]
            ih, il = split(dot_t(pb, slab[...]))
        m = factor_rows(dot_t(wh, p_pad[...]) + dot_t(wl, p_pad[...]) + eye, k)
        mh, ml = split(m)
        if step < ITERS - 1:
            w_high[k : 2 * k, :] = wh
            w_low[k : 2 * k, :] = wl
            current = dot(mh, w_high[...]) + (dot(mh, w_low[...]) + dot(ml, w_high[...]))
        else:
            w_high[k : 2 * k, 0:rows] = ih
            w_low[k : 2 * k, 0:rows] = il
            ih, il = w_high[:, 0:rows], w_low[:, 0:rows]
            basis_ref[...] = (dot(mh, ih) + (dot(mh, il) + dot(ml, ih))) * scale
            factor_ref[...] = jnp.where(col >= row, m, 0.0)[:, 0:k] * (1.0 / scale)


def body(sizes, slab, panel):
    nz, ny, nx = sizes
    rows, d = slab.shape
    k = panel.shape[0]
    scale = math.sqrt(rows * nz * ny * nx * CORES)
    n_sems = 2 * (4 + 4 * 14) + 2 * FAR - 1
    params = functools.partial(pltpu.CompilerParams, vmem_limit_bytes=36 * 1024 * 1024)
    vmem = pl.BlockSpec(memory_space=pltpu.VMEM)

    g_high, g_low, first = pl.pallas_call(
        functools.partial(reduce_kernel, (nz, ny, nx)),
        out_shape=(
            jax.ShapeDtypeStruct((d, d), BF16), jax.ShapeDtypeStruct((d, d), BF16), jax.ShapeDtypeStruct((k, d), F32)
        ),
        in_specs=[vmem] * 2,
        out_specs=(vmem,) * 3,
        scratch_shapes=[
            pltpu.VMEM((CORES, HALF, LANE), F32),
            pltpu.VMEM((HALF, LANE), F32),
            pltpu.VMEM((7, HALF // 8, LANE), F32),
            pltpu.VMEM((7, OWN, LANE), F32),
            pltpu.VMEM((OWN, LANE), F32),
            pltpu.VMEM((FAR, OWN, LANE), F32),
            pltpu.VMEM((OWN, LANE), F32),
            pltpu.VMEM((CORES, HALF, LANE), F32),
            pltpu.SemaphoreType.DMA((n_sems,)),
        ],
        compiler_params=params(collective_id=0, has_side_effects=True),
        cost_estimate=pl.CostEstimate(flops=10**9, bytes_accessed=10**7, transcendentals=0),
    )(slab, panel)
    return pl.pallas_call(
        functools.partial(passes_kernel, scale),
        out_shape=(jax.ShapeDtypeStruct((k, rows), F32), jax.ShapeDtypeStruct((k, k), F32)),
        in_specs=[vmem] * 4,
        out_specs=(vmem,) * 2,
        scratch_shapes=[
            pltpu.VMEM((2 * k, d), BF16),
            pltpu.VMEM((2 * k, d), BF16),
            pltpu.VMEM((2 * k, d), BF16),
        ],
        compiler_params=params(),
        cost_estimate=pl.CostEstimate(flops=2 * 10**9, bytes_accessed=3 * 10**6, transcendentals=0),
    )(slab, g_high, g_low, first)


def solution(mesh):
    nz = mesh.shape["rowa"]
    side = math.isqrt(mesh.shape["rowb"] // CORES)
    in_specs = (P(("rowa", "rowb"), None), P(None, ("rowa", "rowb")))
    out_specs = (P(None, ("rowa", "rowb")), P())
    return jax.shard_map(
        functools.partial(body, (nz, side, side)),
        mesh=mesh, in_specs=in_specs, out_specs=out_specs, check_vma=False,
    )
```

time: 658 us -> 75.4 us (0.11)
  blocking collectives: 612 us -> 0 us
  Pallas kernels: 0 us -> 72.5 us
  other arithmetic: 36.2 us -> 0 us
    psum x6 -> x0, blocking collectives: 612 us -> none  [the longest x3 314 us: body(): projected = lax.psum(partial_sum, ('rowa', 'rowb'))]
    pallas_call x0 -> x2, Pallas kernels: none -> 72.5 us  [the longest x1 62.3 us: body(): pl.pallas_call(functools.partial(reduce_kernel, (nz, ny, nx)), out_shape=...]
    another operation x14 -> x0, other arithmetic: 35.6 us -> none  [the longest x9 19.6 us: body(): lower = jnp.linalg.cholesky(gram)]
where the time goes in v5:
time: 75.4 us; the launch traced here: 75.2 us
  Pallas kernels  72.5 us (96%)
  local copies, waits for them, and re-layouts  2.06 us (3%)
    pallas_call x1, Pallas kernels, body(): pl.pallas_call(functools.partial(reduce_kernel, (nz, ny, nx)), out_shape=...  62.3 us
    pallas_call x1, Pallas kernels, body(): pl.pallas_call(functools.partial(passes_kernel, scale), out_shape=(jax.Sh...  10.2 us
    unnamed x4, local copies, waits for them, and re-layouts  2.06 us

profile of v5, /device:TPU:1, one launch (start us, length us, event | category | flops | bytes accessed | tf_op | source)
XLA Modules:
  0.0 75.2 jit_solution(17197837328615594068)
XLA Ops:
  0.6 0.0 copy-start
  0.6 1.2 %copy-done = bf16[512,1024]{1,0:T(8,128)(2,1)S(1)} copy-done((bf16[512,1024]{1,0:T(8,128)(2,1)S(1)}, bf16[512,1024]{1,0:T(8,128)(2,1)}, u32[]{:S(2)}) %copy-start) | copy-done | bytes 1048600
  1.9 0.0 copy-start.1
  1.9 0.8 %copy-done.1 = bf16[64,512]{1,0:T(8,128)(2,1)S(1)} copy-done((bf16[64,512]{1,0:T(8,128)(2,1)S(1)}, bf16[64,512]{1,0:T(8,128)(2,1)}, u32[]{:S(2)}) %copy-start.1) | copy-done | bytes 65560
  2.7 62.3 %shard_map.41 = (bf16[1024,1024]{1,0:T(8,128)(2,1)S(1)}, bf16[1024,1024]{1,0:T(8,128)(2,1)S(1)}, f32[64,1024]{1,0:T(8,128)S(1)}) custom-call(bf16[512,1024]{1,0:T(8,128)(2,1)S(1)} %copy-done, bf16[64,512]{1,0:T(8,128)(2,1)S(1)} %copy-done.1), custom_call_target="tpu_custom_call" | custom-call | flops 1000000000 | bytes 10000000 | tf_op jit(solution)/shard_map/pallas_call | solution.py:312
  65.0 10.2 %shard_map.42 = (f32[64,512]{1,0:T(8,128)}, f32[64,64]{1,0:T(8,128)}) custom-call(bf16[512,1024]{1,0:T(8,128)(2,1)S(1)} %copy-done, bf16[1024,1024]{1,0:T(8,128)(2,1)S(1)} %get-tuple-element.5.g_high, bf16[1024,1024]{1,0:T(8,128)(2,1)S(1)} %get-tuple-element.6.g_low, f32[64,1024]{1,0:T(8,128)S(1)} %get-tuple-element.7.first), custom_call_target="tpu_custom_call" | custom-call | flops 2000000000 | bytes 3000000 | tf_op jit(solution)/shard_map/pallas_call | solution.py:333
Async XLA Ops:
  0.6 1.2 %copy-start = (bf16[512,1024]{1,0:T(8,128)(2,1)S(1)}, bf16[512,1024]{1,0:T(8,128)(2,1)}, u32[]{:S(2)}) copy-start(bf16[512,1024]{1,0:T(8,128)(2,1)} %slab.3) | copy-start | bytes 3145732
  1.9 0.8 %copy-start.1 = (bf16[64,512]{1,0:T(8,128)(2,1)S(1)}, bf16[64,512]{1,0:T(8,128)(2,1)}, u32[]{:S(2)}) copy-start(bf16[64,512]{1,0:T(8,128)(2,1)} %panel.1) | copy-start | bytes 196612

commit v6 on v5

--- a/solution.py
+++ b/solution.py
@@ -39,10 +39,10 @@
         size = range(PANEL)
         rows = [jnp.broadcast_to(groups[g][s + q : s + q + 1, :], full) for q in size]
         cols = [
-            {i: jnp.broadcast_to(groups[i][:, first + q : first + q + 1], full) for i in range(g, len(groups))}
+            {i: jnp.broadcast_to(groups[i][:, first + q : first + q + 1], full) for i in range(g + 1, len(groups))}
             for q in size
         ]
-        piv = [[jnp.broadcast_to(cols[r][g][s + q : s + q + 1, :], full) for r in size] for q in size]
+        piv = [[jnp.broadcast_to(rows[q][:, first + r : first + r + 1], full) for r in size] for q in size]
         inv = []
         for q in size:
             inv.append(pl.reciprocal(piv[q][q]))
@@ -54,11 +54,10 @@
                 for w in range(r, PANEL):
                     piv[r][w] = piv[r][w] - t * piv[q][w]
             done[g][s + q] = rows[q] * lax.rsqrt(piv[q][q])
-        for i in range(g, len(groups)):
-            new = groups[i]
+        scaled = [rows[q] * inv[q] for q in size]
+        for i in range(g + 1, len(groups)):
             for q in size:
-                new = new - (cols[q][i] * inv[q]) * rows[q]
-            groups[i] = new
+                groups[i] = groups[i] - cols[q][i] * scaled[q]
     sub = lax.broadcasted_iota(jnp.int32, full, 0)
     out = []
     for rows in done:
@@ -69,10 +68,7 @@
     return jnp.concatenate(out, axis=0)
 
 
-JOBS = (
-    (("g", 0, 0, 8), ("g", 3, 3, 8), ("g", 4, 4, 8), ("g", 7, 7, 8), ("p", 0, 4)),
-    (("g", 1, 1, 8), ("g", 2, 2, 8), ("g", 5, 5, 8), ("g", 6, 6, 8), ("p", 4, 8)),
-)
+JOBS = ((("g", 0, 8), ("g", 6, 8), ("p", 0, 4)), (("g", 2, 8), ("g", 4, 8), ("p", 4, 8)))
 SIZES = (12 * LANE, 8 * LANE)
 FIRST = (0, SIZES[0])
 HALF = sum(SIZES)
@@ -85,10 +81,11 @@
 
 def places(cc, k):
     at, out = 0, []
-    for job in JOBS[cc]:
-        for j in range(job[-2], job[-1]):
-            out.append((job[0], job[1] if job[0] == "g" else 0, j, at))
-            at += LANE if job[0] == "g" else k
+    for kind, lo, hi in JOBS[cc]:
+        for i in (lo, lo + 1) if kind == "g" else (0,):
+            for j in range(max(lo, i), hi):
+                out.append((kind, i, j, at))
+                at += LANE if kind == "g" else k
     return out
 
 
@@ -161,22 +158,31 @@
         cp.start()
         sent.append(cp)
 
+    def drain(count):
+        for cp in sent[:count]:
+            cp.wait_send()
+        del sent[:count]
+
     def rows(off, count):
         return pl.ds(off if isinstance(off, int) else pl.multiple_of(off, 8), count)
 
-    for cc in range(CORES):
-        at = 0
-        for job in JOBS[cc]:
-            j0, j1 = job[-2:]
-            if job[0] == "g":
-                left, step = slab[:, job[1] * LANE : (job[1] + 1) * LANE].T, LANE
-            else:
-                left, step = panel[...], k
-            v = dot(left, slab[:, j0 * LANE : j1 * LANE])
-            for j in range(j1 - j0):
-                part[cc, at : at + step, :] = v[:, j * LANE : (j + 1) * LANE]
-                at += step
-
+    def work(half):
+        for cc in range(CORES):
+            @pl.when(half == cc)
+            def _():
+                at = 0
+                for kind, lo, hi in JOBS[cc]:
+                    if kind == "g":
+                        v = dot(slab[:, lo * LANE : (lo + 2) * LANE].T, slab[:, lo * LANE : hi * LANE])
+                    else:
+                        v = dot(panel[...], slab[:, lo * LANE : hi * LANE])
+                    for i in (0, 1) if kind == "g" else (0,):
+                        step = LANE if kind == "g" else k
+                        for j in range(i, hi - lo):
+                            part[cc, at : at + step, :] = v[i * step : (i + 1) * step, j * LANE : (j + 1) * LANE]
+                            at += step
+
+    work(1 - c)
     pl.semaphore_wait(barrier, len(everyone))
 
     streams = range(2)
@@ -186,11 +192,12 @@
     for s in streams:
         where = pl.ds(FIRST[s], SIZES[s])
         start(("c", s), part.at[1 - c, where], got_c.at[where], other)
+    work(c)
     for s in streams:
         started["c", s].wait_recv()
         where = pl.ds(FIRST[s], SIZES[s])
         got_c[where, :] = part[c, where, :] + got_c[where, :]
-        for m in range(1, 8):
+        for m in range(7, 0, -1):
             src = got_c.at[rows(FIRST[s] + index(s, 0, m) * PIECE[s], PIECE[s])]
             start((1, s, m), src, got_1.at[m - 1, pl.ds(FIRST[s] // 8, PIECE[s])], peer(s, 0, m))
     for s in streams:
@@ -199,7 +206,7 @@
             started[1, s, m].wait_recv()
             v = v + got_1[m - 1, FIRST[s] // 8 : FIRST[s] // 8 + PIECE[s], :]
         got_c[rows(off_1[s], PIECE[s]), :] = v
-        for m in range(1, 8):
+        for m in range(7, 0, -1):
             src = got_c.at[rows(off_1[s] + index(s, 1, m) * LAST[s], LAST[s])]
             start((2, s, m), src, got_2.at[m - 1, pl.ds(LAST_AT[s], LAST[s])], peer(s, 1, m))
     for s in streams:
@@ -219,11 +226,12 @@
             device_id=far[q - 1], device_id_type=MESH,
         )
 
+    for q in (2, 1, 3):
+        far_copy(q, me_far).start()
+    got_z[me_far] = own[...]
+    drain(len(sent))
     for q in range(1, FAR):
-        cp = far_copy(q, me_far)
-        cp.start()
-        sent.append(cp)
-    got_z[me_far] = own[...]
+        sent.append(far_copy(q, me_far))
     for q in range(1, FAR):
         far_copy(q, lax.rem(me_far + q, FAR)).wait_recv()
     v = got_z[0]
@@ -233,20 +241,24 @@
 
     for s in streams:
         where = rows(off_2[s], LAST[s])
-        for m in range(1, 8):
+        for m in range(7, 0, -1):
             start((3, s, m), own_t.at[pl.ds(LAST_AT[s], LAST[s])], total.at[c, where], peer(s, 1, m))
         total[c, where, :] = own_t[LAST_AT[s] : LAST_AT[s] + LAST[s], :]
+    before = len(sent)
     for s in streams:
         for m in range(1, 8):
             started[3, s, m].wait_recv()
         where = total.at[c, rows(off_1[s], PIECE[s])]
-        for m in range(1, 8):
+        for m in range(7, 0, -1):
             start((4, s, m), where, where, peer(s, 0, m))
-    for s in streams:
-        for m in range(1, 8):
-            started[4, s, m].wait_recv()
-        where = total.at[c, pl.ds(FIRST[s], SIZES[s])]
-        start((5, s), where, where, other)
+    drain(before)
+    for s in streams:
+        for part_at, masks in enumerate((range(1, 4), range(4, 8))):
+            for m in masks:
+                started[4, s, m].wait_recv()
+            begin = FIRST[s] + flip(z_low, part_at) * 4 * PIECE[s]
+            where = total.at[c, rows(begin, 4 * PIECE[s])]
+            start((5, s, part_at), where, where, other)
 
     def whole(half):
         for cc in range(CORES):
@@ -263,11 +275,12 @@
                         g_low[a * LANE : (a + 1) * LANE, e * LANE : (e + 1) * LANE] = low
 
     whole(c)
-    for s in streams:
-        started[5, s].wait_recv()
+    drain(len(sent) - 4)
+    for s in streams:
+        for part_at in range(2):
+            started[5, s, part_at].wait_recv()
     whole(1 - c)
-    for cp in sent:
-        cp.wait_send()
+    drain(len(sent))
 
 
 def passes_kernel(scale, slab, g_high, g_low, first, basis_ref, factor_ref, w_high, w_low, p_pad):
@@ -305,7 +318,7 @@
     rows, d = slab.shape
     k = panel.shape[0]
     scale = math.sqrt(rows * nz * ny * nx * CORES)
-    n_sems = 2 * (4 + 4 * 14) + 2 * FAR - 1
+    n_sems = 2 * (6 + 4 * 14) + 2 * FAR - 1
     params = functools.partial(pltpu.CompilerParams, vmem_limit_bytes=36 * 1024 * 1024)
     vmem = pl.BlockSpec(memory_space=pltpu.VMEM)
 

time: 75.4 us -> 72.3 us (0.959)
  Pallas kernels: 72.5 us -> 69.4 us
    pallas_call x1, Pallas kernels: 62.3 us -> 59.2 us  [body(): pl.pallas_call(functools.partial(reduce_kernel, (nz, ny, nx)), out_shape=...]
where the time goes in v6:
time: 72.3 us; the launch traced here: 72.1 us
  Pallas kernels  69.4 us (96%)
  local copies, waits for them, and re-layouts  2.06 us (3%)
    pallas_call x1, Pallas kernels, body(): pl.pallas_call(functools.partial(reduce_kernel, (nz, ny, nx)), out_shape=...  59.2 us
    pallas_call x1, Pallas kernels, body(): pl.pallas_call(functools.partial(passes_kernel, scale), out_shape=(jax.Sh...  10.2 us
    unnamed x4, local copies, waits for them, and re-layouts  2.06 us

profile of v6, /device:TPU:1, one launch (start us, length us, event | category | flops | bytes accessed | tf_op | source)
XLA Modules:
  0.0 72.1 jit_solution(16373082047676362289)
XLA Ops:
  0.6 0.0 copy-start
  0.6 1.2 %copy-done = bf16[512,1024]{1,0:T(8,128)(2,1)S(1)} copy-done((bf16[512,1024]{1,0:T(8,128)(2,1)S(1)}, bf16[512,1024]{1,0:T(8,128)(2,1)}, u32[]{:S(2)}) %copy-start) | copy-done | bytes 1048600
  1.9 0.0 copy-start.1
  1.9 0.8 %copy-done.1 = bf16[64,512]{1,0:T(8,128)(2,1)S(1)} copy-done((bf16[64,512]{1,0:T(8,128)(2,1)S(1)}, bf16[64,512]{1,0:T(8,128)(2,1)}, u32[]{:S(2)}) %copy-start.1) | copy-done | bytes 65560
  2.7 59.2 %shard_map.41 = (bf16[1024,1024]{1,0:T(8,128)(2,1)S(1)}, bf16[1024,1024]{1,0:T(8,128)(2,1)S(1)}, f32[64,1024]{1,0:T(8,128)S(1)}) custom-call(bf16[512,1024]{1,0:T(8,128)(2,1)S(1)} %copy-done, bf16[64,512]{1,0:T(8,128)(2,1)S(1)} %copy-done.1), custom_call_target="tpu_custom_call" | custom-call | flops 1000000000 | bytes 10000000 | tf_op jit(solution)/shard_map/pallas_call | solution.py:325
  62.0 10.2 %shard_map.42 = (f32[64,512]{1,0:T(8,128)}, f32[64,64]{1,0:T(8,128)}) custom-call(bf16[512,1024]{1,0:T(8,128)(2,1)S(1)} %copy-done, bf16[1024,1024]{1,0:T(8,128)(2,1)S(1)} %get-tuple-element.5.g_high, bf16[1024,1024]{1,0:T(8,128)(2,1)S(1)} %get-tuple-element.6.g_low, f32[64,1024]{1,0:T(8,128)S(1)} %get-tuple-element.7.first), custom_call_target="tpu_custom_call" | custom-call | flops 2000000000 | bytes 3000000 | tf_op jit(solution)/shard_map/pallas_call | solution.py:346
Async XLA Ops:
  0.6 1.2 %copy-start = (bf16[512,1024]{1,0:T(8,128)(2,1)S(1)}, bf16[512,1024]{1,0:T(8,128)(2,1)}, u32[]{:S(2)}) copy-start(bf16[512,1024]{1,0:T(8,128)(2,1)} %slab.3) | copy-start | bytes 3145732
  1.9 0.8 %copy-start.1 = (bf16[64,512]{1,0:T(8,128)(2,1)S(1)}, bf16[64,512]{1,0:T(8,128)(2,1)}, u32[]{:S(2)}) copy-start(bf16[64,512]{1,0:T(8,128)(2,1)} %panel.1) | copy-start | bytes 196612

commit v7 on v6

--- a/solution.py
+++ b/solution.py
@@ -93,9 +93,11 @@
     return bit + mask - 2 * bit * mask
 
 
-def reduce_kernel(dims, slab, panel, g_high, g_low, first, part, got_c, got_1, got_2, own, got_z, own_t, total, sems):
+def reduce_kernel(dims, slab, panel, g_high, g_low, first, part, got_c, got_1a, got_1b,
+                  got_2a, got_2b, own, got_z, own_t, total, sems):
     nz, ny, nx = dims
     k = panel.shape[0]
+    got_1, got_2 = (got_1a, got_1b), (got_2a, got_2b)
 
     z = lax.axis_index("rowa")
     b = lax.axis_index("rowb")
@@ -148,14 +150,18 @@
 
     used, sent, started = [0], [], {}
 
-    def start(key, src, dst, device_id):
-        at = used[0]
-        used[0] += 2
-        cp = started[key] = pltpu.make_async_remote_copy(
+    def copy(src, dst, at, device_id):
+        return pltpu.make_async_remote_copy(
             src_ref=src, dst_ref=dst, send_sem=sems.at[at], recv_sem=sems.at[at + 1],
             device_id=device_id, device_id_type=MESH,
         )
-        cp.start()
+
+    def start(key, copies, everything):
+        at = used[0]
+        used[0] += 2
+        for src, dst, device_id in copies:
+            copy(src, dst, at, device_id).start()
+        cp = started[key] = copy(everything, everything, at, other)
         sent.append(cp)
 
     def drain(count):
@@ -191,29 +197,33 @@
 
     for s in streams:
         where = pl.ds(FIRST[s], SIZES[s])
-        start(("c", s), part.at[1 - c, where], got_c.at[where], other)
+        start(("c", s), [(part.at[1 - c, where], got_c.at[where], other)], got_c.at[where])
     work(c)
     for s in streams:
         started["c", s].wait_recv()
         where = pl.ds(FIRST[s], SIZES[s])
         got_c[where, :] = part[c, where, :] + got_c[where, :]
-        for m in range(7, 0, -1):
-            src = got_c.at[rows(FIRST[s] + index(s, 0, m) * PIECE[s], PIECE[s])]
-            start((1, s, m), src, got_1.at[m - 1, pl.ds(FIRST[s] // 8, PIECE[s])], peer(s, 0, m))
-    for s in streams:
+        copies = [
+            (got_c.at[rows(FIRST[s] + index(s, 0, m) * PIECE[s], PIECE[s])], got_1[s].at[m - 1], peer(s, 0, m))
+            for m in range(7, 0, -1)
+        ]
+        start((1, s), copies, got_1[s])
+    for s in streams:
+        started[1, s].wait_recv()
         v = got_c[rows(off_1[s], PIECE[s]), :]
         for m in range(1, 8):
-            started[1, s, m].wait_recv()
-            v = v + got_1[m - 1, FIRST[s] // 8 : FIRST[s] // 8 + PIECE[s], :]
+            v = v + got_1[s][m - 1]
         got_c[rows(off_1[s], PIECE[s]), :] = v
-        for m in range(7, 0, -1):
-            src = got_c.at[rows(off_1[s] + index(s, 1, m) * LAST[s], LAST[s])]
-            start((2, s, m), src, got_2.at[m - 1, pl.ds(LAST_AT[s], LAST[s])], peer(s, 1, m))
-    for s in streams:
+        copies = [
+            (got_c.at[rows(off_1[s] + index(s, 1, m) * LAST[s], LAST[s])], got_2[s].at[m - 1], peer(s, 1, m))
+            for m in range(7, 0, -1)
+        ]
+        start((2, s), copies, got_2[s])
+    for s in streams:
+        started[2, s].wait_recv()
         v = got_c[rows(off_2[s], LAST[s]), :]
         for m in range(1, 8):
-            started[2, s, m].wait_recv()
-            v = v + got_2[m - 1, LAST_AT[s] : LAST_AT[s] + LAST[s], :]
+            v = v + got_2[s][m - 1]
         own[LAST_AT[s] : LAST_AT[s] + LAST[s], :] = v
 
     me_far = z // (nz // FAR)
@@ -241,30 +251,32 @@
 
     for s in streams:
         where = rows(off_2[s], LAST[s])
-        for m in range(7, 0, -1):
-            start((3, s, m), own_t.at[pl.ds(LAST_AT[s], LAST[s])], total.at[c, where], peer(s, 1, m))
+        src = own_t.at[pl.ds(LAST_AT[s], LAST[s])]
+        copies = [(src, total.at[c, where], peer(s, 1, m)) for m in range(7, 0, -1)]
+        start((3, s), copies, total.at[c, pl.ds(FIRST[s], 7 * LAST[s])])
         total[c, where, :] = own_t[LAST_AT[s] : LAST_AT[s] + LAST[s], :]
     before = len(sent)
     for s in streams:
-        for m in range(1, 8):
-            started[3, s, m].wait_recv()
+        started[3, s].wait_recv()
         where = total.at[c, rows(off_1[s], PIECE[s])]
-        for m in range(7, 0, -1):
-            start((4, s, m), where, where, peer(s, 0, m))
+        for part_at, masks in enumerate(((3, 2, 1), (7, 6, 5, 4))):
+            copies = [(where, where, peer(s, 0, m)) for m in masks]
+            start((4, s, part_at), copies, total.at[c, pl.ds(FIRST[s], len(masks) * PIECE[s])])
     drain(before)
     for s in streams:
-        for part_at, masks in enumerate((range(1, 4), range(4, 8))):
-            for m in masks:
-                started[4, s, m].wait_recv()
+        for part_at in range(2):
+            started[4, s, part_at].wait_recv()
             begin = FIRST[s] + flip(z_low, part_at) * 4 * PIECE[s]
             where = total.at[c, rows(begin, 4 * PIECE[s])]
-            start((5, s, part_at), where, where, other)
-
-    def whole(half):
+            start((5, s, part_at), [(where, where, other)], where)
+
+    def whole(half, s):
         for cc in range(CORES):
             @pl.when(half == cc)
             def _():
                 for kind, i, j, at in places(cc, k):
+                    if (at >= SIZES[0]) != s:
+                        continue
                     if kind == "p":
                         first[:, j * LANE : (j + 1) * LANE] = total[cc, at : at + k, :]
                         continue
@@ -274,16 +286,17 @@
                         g_high[a * LANE : (a + 1) * LANE, e * LANE : (e + 1) * LANE] = high
                         g_low[a * LANE : (a + 1) * LANE, e * LANE : (e + 1) * LANE] = low
 
-    whole(c)
+    for s in streams:
+        whole(c, s)
     drain(len(sent) - 4)
     for s in streams:
         for part_at in range(2):
             started[5, s, part_at].wait_recv()
-    whole(1 - c)
+        whole(1 - c, s)
     drain(len(sent))
 
 
-def passes_kernel(scale, slab, g_high, g_low, first, basis_ref, factor_ref, w_high, w_low, p_pad):
+def passes_kernel(scale, slab, g_high, g_low, first, basis_ref, factor_ref, w_high, w_low, w_both, p_pad):
     k, d = first.shape
     w_high[0:k, :] = jnp.zeros((k, d), BF16)
     w_low[0:k, :] = jnp.zeros((k, d), BF16)
@@ -299,12 +312,16 @@
         if step == ITERS - 1:
             rows = slab.shape[0]
             ih, il = split(dot_t(pb, slab[...]))
-        m = factor_rows(dot_t(wh, p_pad[...]) + dot_t(wl, p_pad[...]) + eye, k)
+        w_both[0:k, :] = wh
+        w_both[k : 2 * k, :] = wl
+        gram = dot_t(w_both[...], p_pad[...])
+        m = factor_rows(gram[0:k, :] + gram[k : 2 * k, :] + eye, k)
         mh, ml = split(m)
         if step < ITERS - 1:
             w_high[k : 2 * k, :] = wh
             w_low[k : 2 * k, :] = wl
-            current = dot(mh, w_high[...]) + (dot(mh, w_low[...]) + dot(ml, w_high[...]))
+            both = dot(jnp.concatenate([mh, ml], axis=0), w_high[...])
+            current = both[0:k, :] + (dot(mh, w_low[...]) + both[k : 2 * k, :])
         else:
             w_high[k : 2 * k, 0:rows] = ih
             w_low[k : 2 * k, 0:rows] = il
@@ -318,7 +335,7 @@
     rows, d = slab.shape
     k = panel.shape[0]
     scale = math.sqrt(rows * nz * ny * nx * CORES)
-    n_sems = 2 * (6 + 4 * 14) + 2 * FAR - 1
+    n_sems = 2 * 16 + 2 * FAR - 1
     params = functools.partial(pltpu.CompilerParams, vmem_limit_bytes=36 * 1024 * 1024)
     vmem = pl.BlockSpec(memory_space=pltpu.VMEM)
 
@@ -332,8 +349,7 @@
         scratch_shapes=[
             pltpu.VMEM((CORES, HALF, LANE), F32),
             pltpu.VMEM((HALF, LANE), F32),
-            pltpu.VMEM((7, HALF // 8, LANE), F32),
-            pltpu.VMEM((7, OWN, LANE), F32),
+            *[pltpu.VMEM((7, size, LANE), F32) for size in PIECE + LAST],
             pltpu.VMEM((OWN, LANE), F32),
             pltpu.VMEM((FAR, OWN, LANE), F32),
             pltpu.VMEM((OWN, LANE), F32),
@@ -352,6 +368,7 @@
             pltpu.VMEM((2 * k, d), BF16),
             pltpu.VMEM((2 * k, d), BF16),
             pltpu.VMEM((2 * k, d), BF16),
+            pltpu.VMEM((2 * k, d), BF16),
         ],
         compiler_params=params(),
         cost_estimate=pl.CostEstimate(flops=2 * 10**9, bytes_accessed=3 * 10**6, transcendentals=0),

time: 72.3 us -> 71 us (0.982)
  Pallas kernels: 69.4 us -> 68.1 us
    pallas_call x1, Pallas kernels: 59.2 us -> 58.2 us  [body(): pl.pallas_call(functools.partial(reduce_kernel, (nz, ny, nx)), out_shape=...]
where the time goes in v7:
time: 71 us; the launch traced here: 70.8 us
  Pallas kernels  68.1 us (96%)
  local copies, waits for them, and re-layouts  2.06 us (3%)
    pallas_call x1, Pallas kernels, body(): pl.pallas_call(functools.partial(reduce_kernel, (nz, ny, nx)), out_shape=...  58.2 us
    pallas_call x1, Pallas kernels, body(): pl.pallas_call(functools.partial(passes_kernel, scale), out_shape=(jax.Sh...  9.97 us
    unnamed x4, local copies, waits for them, and re-layouts  2.06 us

profile of v7, /device:TPU:1, one launch (start us, length us, event | category | flops | bytes accessed | tf_op | source)
XLA Modules:
  0.0 70.8 jit_solution(14096807873651524881)
XLA Ops:
  0.6 0.0 copy-start
  0.6 1.2 %copy-done = bf16[512,1024]{1,0:T(8,128)(2,1)S(1)} copy-done((bf16[512,1024]{1,0:T(8,128)(2,1)S(1)}, bf16[512,1024]{1,0:T(8,128)(2,1)}, u32[]{:S(2)}) %copy-start) | copy-done | bytes 1048600
  1.9 0.0 copy-start.1
  1.9 0.8 %copy-done.1 = bf16[64,512]{1,0:T(8,128)(2,1)S(1)} copy-done((bf16[64,512]{1,0:T(8,128)(2,1)S(1)}, bf16[64,512]{1,0:T(8,128)(2,1)}, u32[]{:S(2)}) %copy-start.1) | copy-done | bytes 65560
  2.7 58.2 %shard_map.41 = (bf16[1024,1024]{1,0:T(8,128)(2,1)S(1)}, bf16[1024,1024]{1,0:T(8,128)(2,1)S(1)}, f32[64,1024]{1,0:T(8,128)S(1)}) custom-call(bf16[512,1024]{1,0:T(8,128)(2,1)S(1)} %copy-done, bf16[64,512]{1,0:T(8,128)(2,1)S(1)} %copy-done.1), custom_call_target="tpu_custom_call" | custom-call | flops 1000000000 | bytes 10000000 | tf_op jit(solution)/shard_map/pallas_call | solution.py:342
  60.9 10.0 %shard_map.42 = (f32[64,512]{1,0:T(8,128)}, f32[64,64]{1,0:T(8,128)}) custom-call(bf16[512,1024]{1,0:T(8,128)(2,1)S(1)} %copy-done, bf16[1024,1024]{1,0:T(8,128)(2,1)S(1)} %get-tuple-element.5.g_high, bf16[1024,1024]{1,0:T(8,128)(2,1)S(1)} %get-tuple-element.6.g_low, f32[64,1024]{1,0:T(8,128)S(1)} %get-tuple-element.7.first), custom_call_target="tpu_custom_call" | custom-call | flops 2000000000 | bytes 3000000 | tf_op jit(solution)/shard_map/pallas_call | solution.py:362
Async XLA Ops:
  0.6 1.2 %copy-start = (bf16[512,1024]{1,0:T(8,128)(2,1)S(1)}, bf16[512,1024]{1,0:T(8,128)(2,1)}, u32[]{:S(2)}) copy-start(bf16[512,1024]{1,0:T(8,128)(2,1)} %slab.3) | copy-start | bytes 3145732
  1.9 0.8 %copy-start.1 = (bf16[64,512]{1,0:T(8,128)(2,1)S(1)}, bf16[64,512]{1,0:T(8,128)(2,1)}, u32[]{:S(2)}) copy-start(bf16[64,512]{1,0:T(8,128)(2,1)} %panel.1) | copy-start | bytes 196612

commit v8 on v7

--- a/solution.py
+++ b/solution.py
@@ -68,7 +68,8 @@
     return jnp.concatenate(out, axis=0)
 
 
-JOBS = ((("g", 0, 8), ("g", 6, 8), ("p", 0, 4)), (("g", 2, 8), ("g", 4, 8), ("p", 4, 8)))
+JOBS = ((("g", 0, 8), ("g", 6, 8), ("p", 0, 4)), (("g", 2, 8), ("p", 4, 8), ("g", 4, 8)))
+EARLY = (1, 2)
 SIZES = (12 * LANE, 8 * LANE)
 FIRST = (0, SIZES[0])
 HALF = sum(SIZES)
@@ -94,7 +95,7 @@
 
 
 def reduce_kernel(dims, slab, panel, g_high, g_low, first, part, got_c, got_1a, got_1b,
-                  got_2a, got_2b, own, got_z, own_t, total, sems):
+                  got_2a, got_2b, own, got_z, own_t, total, known, sems):
     nz, ny, nx = dims
     k = panel.shape[0]
     got_1, got_2 = (got_1a, got_1b), (got_2a, got_2b)
@@ -143,10 +144,14 @@
     far = [device(lax.rem(z + q * (nz // FAR), nz), y, x, c) for q in range(1, FAR)]
 
     barrier = pltpu.get_barrier_semaphore()
-    everyone = far + [other] + [peer(s, 0, m) for s in range(2) for m in range(1, 8)]
+    everyone = [other] + [peer(s, 0, m) for s in range(2) for m in range(1, 8)]
     everyone += [peer(s, 1, m) for s in range(2) for m in range(4, 8)]
     for device_id in everyone:
         pl.semaphore_signal(barrier, inc=1, device_id=device_id, device_id_type=MESH)
+
+    def tell(level, devices):
+        for device_id in devices:
+            pl.semaphore_signal(known.at[level], inc=1, device_id=device_id, device_id_type=MESH)
 
     used, sent, started = [0], [], {}
 
@@ -172,34 +177,37 @@
     def rows(off, count):
         return pl.ds(off if isinstance(off, int) else pl.multiple_of(off, 8), count)
 
-    def work(half):
+    def work(half, stream):
         for cc in range(CORES):
             @pl.when(half == cc)
             def _():
                 at = 0
-                for kind, lo, hi in JOBS[cc]:
-                    if kind == "g":
+                for number, (kind, lo, hi) in enumerate(JOBS[cc]):
+                    mine = (number >= EARLY[cc]) == stream
+                    if mine and kind == "g":
                         v = dot(slab[:, lo * LANE : (lo + 2) * LANE].T, slab[:, lo * LANE : hi * LANE])
-                    else:
+                    elif mine:
                         v = dot(panel[...], slab[:, lo * LANE : hi * LANE])
                     for i in (0, 1) if kind == "g" else (0,):
                         step = LANE if kind == "g" else k
                         for j in range(i, hi - lo):
-                            part[cc, at : at + step, :] = v[i * step : (i + 1) * step, j * LANE : (j + 1) * LANE]
+                            if mine:
+                                part[cc, at : at + step, :] = v[i * step : (i + 1) * step, j * LANE : (j + 1) * LANE]
                             at += step
-
-    work(1 - c)
-    pl.semaphore_wait(barrier, len(everyone))
 
     streams = range(2)
     off_1 = [FIRST[s] + index(s, 0, 0) * PIECE[s] for s in streams]
     off_2 = [off_1[s] + index(s, 1, 0) * LAST[s] for s in streams]
 
     for s in streams:
+        work(1 - c, s)
+        if s == 0:
+            pl.semaphore_wait(barrier, len(everyone))
         where = pl.ds(FIRST[s], SIZES[s])
         start(("c", s), [(part.at[1 - c, where], got_c.at[where], other)], got_c.at[where])
-    work(c)
-    for s in streams:
+    tell(0, [peer(s, 1, 4) for s in streams])
+    for s in streams:
+        work(c, s)
         started["c", s].wait_recv()
         where = pl.ds(FIRST[s], SIZES[s])
         got_c[where, :] = part[c, where, :] + got_c[where, :]
@@ -208,6 +216,8 @@
             for m in range(7, 0, -1)
         ]
         start((1, s), copies, got_1[s])
+    pl.semaphore_wait(known.at[0], 2)
+    tell(1, [far[0], far[2]])
     for s in streams:
         started[1, s].wait_recv()
         v = got_c[rows(off_1[s], PIECE[s]), :]
@@ -236,6 +246,7 @@
             device_id=far[q - 1], device_id_type=MESH,
         )
 
+    pl.semaphore_wait(known.at[1], 2)
     for q in (2, 1, 3):
         far_copy(q, me_far).start()
     got_z[me_far] = own[...]
@@ -354,6 +365,7 @@
             pltpu.VMEM((FAR, OWN, LANE), F32),
             pltpu.VMEM((OWN, LANE), F32),
             pltpu.VMEM((CORES, HALF, LANE), F32),
+            pltpu.SemaphoreType.REGULAR((2,)),
             pltpu.SemaphoreType.DMA((n_sems,)),
         ],
         compiler_params=params(collective_id=0, has_side_effects=True),

time: 71 us -> 71.2 us (level)
  no operation moved by 1% of the time
where the time goes in v8:
time: 71.2 us; the launch traced here: 71 us
  Pallas kernels  68.3 us (96%)
  local copies, waits for them, and re-layouts  2.06 us (3%)
    pallas_call x1, Pallas kernels, body(): pl.pallas_call(functools.partial(reduce_kernel, (nz, ny, nx)), out_shape=...  58.3 us
    pallas_call x1, Pallas kernels, body(): pl.pallas_call(functools.partial(passes_kernel, scale), out_shape=(jax.Sh...  9.98 us
    unnamed x4, local copies, waits for them, and re-layouts  2.06 us

profile of v8, /device:TPU:1, one launch (start us, length us, event | category | flops | bytes accessed | tf_op | source)
XLA Modules:
  0.0 71.0 jit_solution(9432819926322470045)
XLA Ops:
  0.6 0.0 copy-start
  0.6 1.2 %copy-done = bf16[512,1024]{1,0:T(8,128)(2,1)S(1)} copy-done((bf16[512,1024]{1,0:T(8,128)(2,1)S(1)}, bf16[512,1024]{1,0:T(8,128)(2,1)}, u32[]{:S(2)}) %copy-start) | copy-done | bytes 1048600
  1.9 0.0 copy-start.1
  1.9 0.8 %copy-done.1 = bf16[64,512]{1,0:T(8,128)(2,1)S(1)} copy-done((bf16[64,512]{1,0:T(8,128)(2,1)S(1)}, bf16[64,512]{1,0:T(8,128)(2,1)}, u32[]{:S(2)}) %copy-start.1) | copy-done | bytes 65560
  2.7 58.3 %shard_map.41 = (bf16[1024,1024]{1,0:T(8,128)(2,1)S(1)}, bf16[1024,1024]{1,0:T(8,128)(2,1)S(1)}, f32[64,1024]{1,0:T(8,128)S(1)}) custom-call(bf16[512,1024]{1,0:T(8,128)(2,1)S(1)} %copy-done, bf16[64,512]{1,0:T(8,128)(2,1)S(1)} %copy-done.1), custom_call_target="tpu_custom_call" | custom-call | flops 1000000000 | bytes 10000000 | tf_op jit(solution)/shard_map/pallas_call | solution.py:353
  61.0 10.0 %shard_map.42 = (f32[64,512]{1,0:T(8,128)}, f32[64,64]{1,0:T(8,128)}) custom-call(bf16[512,1024]{1,0:T(8,128)(2,1)S(1)} %copy-done, bf16[1024,1024]{1,0:T(8,128)(2,1)S(1)} %get-tuple-element.5.g_high, bf16[1024,1024]{1,0:T(8,128)(2,1)S(1)} %get-tuple-element.6.g_low, f32[64,1024]{1,0:T(8,128)S(1)} %get-tuple-element.7.first), custom_call_target="tpu_custom_call" | custom-call | flops 2000000000 | bytes 3000000 | tf_op jit(solution)/shard_map/pallas_call | solution.py:374
Async XLA Ops:
  0.6 1.2 %copy-start = (bf16[512,1024]{1,0:T(8,128)(2,1)S(1)}, bf16[512,1024]{1,0:T(8,128)(2,1)}, u32[]{:S(2)}) copy-start(bf16[512,1024]{1,0:T(8,128)(2,1)} %slab.3) | copy-start | bytes 3145732
  1.9 0.8 %copy-start.1 = (bf16[64,512]{1,0:T(8,128)(2,1)S(1)}, bf16[64,512]{1,0:T(8,128)(2,1)}, u32[]{:S(2)}) copy-start(bf16[64,512]{1,0:T(8,128)(2,1)} %panel.1) | copy-start | bytes 196612

commit v9 on v8

--- a/solution.py
+++ b/solution.py
@@ -69,14 +69,10 @@
 
 
 JOBS = ((("g", 0, 8), ("g", 6, 8), ("p", 0, 4)), (("g", 2, 8), ("p", 4, 8), ("g", 4, 8)))
-EARLY = (1, 2)
-SIZES = (12 * LANE, 8 * LANE)
-FIRST = (0, SIZES[0])
-HALF = sum(SIZES)
-PIECE = tuple(size // 8 for size in SIZES)
-LAST = tuple(size // 64 for size in SIZES)
-LAST_AT = (0, LAST[0])
-OWN = sum(LAST)
+EARLY = (1, 1)
+ROWS = 20 * LANE
+PIECE = ROWS // 8
+OWN = PIECE // 8
 FAR = 4
 
 
@@ -94,11 +90,9 @@
     return bit + mask - 2 * bit * mask
 
 
-def reduce_kernel(dims, slab, panel, g_high, g_low, first, part, got_c, got_1a, got_1b,
-                  got_2a, got_2b, own, got_z, own_t, total, known, sems):
+def reduce_kernel(dims, slab, panel, g_high, g_low, first, part, got_c, got_1, got_2, own, got_z, own_t, total, known, sems):
     nz, ny, nx = dims
     k = panel.shape[0]
-    got_1, got_2 = (got_1a, got_1b), (got_2a, got_2b)
 
     z = lax.axis_index("rowa")
     b = lax.axis_index("rowb")
@@ -124,28 +118,31 @@
     def pick(pair, family):
         return tuple(a + family * (e - a) for a, e in zip(*pair))
 
-    families = [lax.rem(s + c, 2) for s in range(2)]
-    groups = [
-        (
-            [pick(pair, f) for pair in (pair_x, pair_y, pair_z)],
-            [pick(pair_x, 1 - f), pick(pair_y, 1 - f), pick(pair_z2, f)],
-        )
-        for f in families
-    ]
-
-    def peer(s, step, mask):
-        px, py, pz = groups[s][step]
+    groups = (
+        [pick(pair, c) for pair in (pair_x, pair_y, pair_z)],
+        [pick(pair_x, 1 - c), pick(pair_y, 1 - c), pick(pair_z2, c)],
+    )
+    others = (
+        [pick(pair, 1 - c) for pair in (pair_x, pair_y, pair_z)],
+        [pick(pair_x, c), pick(pair_y, c), pick(pair_z2, 1 - c)],
+    )
+
+    def member(group, mask):
+        px, py, pz = group
         return device(pz[1] if mask & 4 else z, py[1] if mask & 2 else y, px[1] if mask & 1 else x, c)
 
-    def index(s, step, mask):
-        return sum(flip(bit, mask >> i & 1) * (1 << i) for i, (bit, _) in enumerate(groups[s][step]))
+    def peer(step, mask):
+        return member(groups[step], mask)
+
+    def index(step, mask):
+        return sum(flip(bit, mask >> i & 1) * (1 << i) for i, (bit, _) in enumerate(groups[step]))
 
     other = device(z, y, x, 1 - c)
     far = [device(lax.rem(z + q * (nz // FAR), nz), y, x, c) for q in range(1, FAR)]
 
     barrier = pltpu.get_barrier_semaphore()
-    everyone = [other] + [peer(s, 0, m) for s in range(2) for m in range(1, 8)]
-    everyone += [peer(s, 1, m) for s in range(2) for m in range(4, 8)]
+    near_z2 = [member(group[1], 4) for group in (groups, others)]
+    everyone = [other] + [peer(0, m) for m in range(1, 8)] + [peer(1, m) for m in range(1, 8)] + near_z2[1:]
     for device_id in everyone:
         pl.semaphore_signal(barrier, inc=1, device_id=device_id, device_id_type=MESH)
 
@@ -177,13 +174,13 @@
     def rows(off, count):
         return pl.ds(off if isinstance(off, int) else pl.multiple_of(off, 8), count)
 
-    def work(half, stream):
+    def work(half, later):
         for cc in range(CORES):
             @pl.when(half == cc)
             def _():
                 at = 0
                 for number, (kind, lo, hi) in enumerate(JOBS[cc]):
-                    mine = (number >= EARLY[cc]) == stream
+                    mine = (number >= EARLY[cc]) == later
                     if mine and kind == "g":
                         v = dot(slab[:, lo * LANE : (lo + 2) * LANE].T, slab[:, lo * LANE : hi * LANE])
                     elif mine:
@@ -195,46 +192,50 @@
                                 part[cc, at : at + step, :] = v[i * step : (i + 1) * step, j * LANE : (j + 1) * LANE]
                             at += step
 
-    streams = range(2)
-    off_1 = [FIRST[s] + index(s, 0, 0) * PIECE[s] for s in streams]
-    off_2 = [off_1[s] + index(s, 1, 0) * LAST[s] for s in streams]
-
-    for s in streams:
-        work(1 - c, s)
-        if s == 0:
+    off_1 = index(0, 0) * PIECE
+    off_2 = off_1 + index(1, 0) * OWN
+    halves = [pl.ds(h * ROWS // 2, ROWS // 2) for h in range(2)]
+
+    for h in range(2):
+        work(1 - c, h)
+        if h == 0:
             pl.semaphore_wait(barrier, len(everyone))
-        where = pl.ds(FIRST[s], SIZES[s])
-        start(("c", s), [(part.at[1 - c, where], got_c.at[where], other)], got_c.at[where])
-    tell(0, [peer(s, 1, 4) for s in streams])
-    for s in streams:
-        work(c, s)
-        started["c", s].wait_recv()
-        where = pl.ds(FIRST[s], SIZES[s])
-        got_c[where, :] = part[c, where, :] + got_c[where, :]
-        copies = [
-            (got_c.at[rows(FIRST[s] + index(s, 0, m) * PIECE[s], PIECE[s])], got_1[s].at[m - 1], peer(s, 0, m))
-            for m in range(7, 0, -1)
-        ]
-        start((1, s), copies, got_1[s])
+        start(("c", h), [(part.at[1 - c, halves[h]], got_c.at[halves[h]], other)], got_c.at[halves[h]])
+    tell(0, near_z2)
+    at_1 = used[0]
+    used[0] += 2
+    for h in range(2):
+        work(c, h)
+        started["c", h].wait_recv()
+        got_c[halves[h], :] = part[c, halves[h], :] + got_c[halves[h], :]
+        cross = flip(z_low, h)
+        z_to = z + cross * (groups[0][2][1] - z)
+        for m in (3, 2, 1, 0):
+            px, py, _ = groups[0]
+            to = device(z_to, py[1] if m & 2 else y, px[1] if m & 1 else x, c)
+            first_row = (flip(px[0], m & 1) + 2 * flip(py[0], m >> 1) + 4 * h) * PIECE
+            slot = m - 1 + 4 * cross if m else 3
+            send = copy(got_c.at[rows(first_row, PIECE)], got_1.at[slot], at_1, to)
+            if m:
+                send.start()
+            else:
+                pl.when(cross == 1)(send.start)
+    started[1] = copy(got_1, got_1, at_1, other)
+    sent.append(started[1])
     pl.semaphore_wait(known.at[0], 2)
     tell(1, [far[0], far[2]])
-    for s in streams:
-        started[1, s].wait_recv()
-        v = got_c[rows(off_1[s], PIECE[s]), :]
-        for m in range(1, 8):
-            v = v + got_1[s][m - 1]
-        got_c[rows(off_1[s], PIECE[s]), :] = v
-        copies = [
-            (got_c.at[rows(off_1[s] + index(s, 1, m) * LAST[s], LAST[s])], got_2[s].at[m - 1], peer(s, 1, m))
-            for m in range(7, 0, -1)
-        ]
-        start((2, s), copies, got_2[s])
-    for s in streams:
-        started[2, s].wait_recv()
-        v = got_c[rows(off_2[s], LAST[s]), :]
-        for m in range(1, 8):
-            v = v + got_2[s][m - 1]
-        own[LAST_AT[s] : LAST_AT[s] + LAST[s], :] = v
+    started[1].wait_recv()
+    v = got_c[rows(off_1, PIECE), :]
+    for m in range(1, 8):
+        v = v + got_1[m - 1]
+    got_c[rows(off_1, PIECE), :] = v
+    copies = [(got_c.at[rows(off_1 + index(1, m) * OWN, OWN)], got_2.at[m - 1], peer(1, m)) for m in range(7, 0, -1)]
+    start(2, copies, got_2)
+    started[2].wait_recv()
+    v = got_c[rows(off_2, OWN), :]
+    for m in range(1, 8):
+        v = v + got_2[m - 1]
+    own[...] = v
 
     me_far = z // (nz // FAR)
     send_z, recv_z = used[0], used[0] + FAR - 1
@@ -260,50 +261,43 @@
         v = v + got_z[q]
     own_t[...] = v
 
-    for s in streams:
-        where = rows(off_2[s], LAST[s])
-        src = own_t.at[pl.ds(LAST_AT[s], LAST[s])]
-        copies = [(src, total.at[c, where], peer(s, 1, m)) for m in range(7, 0, -1)]
-        start((3, s), copies, total.at[c, pl.ds(FIRST[s], 7 * LAST[s])])
-        total[c, where, :] = own_t[LAST_AT[s] : LAST_AT[s] + LAST[s], :]
+    where = total.at[c, rows(off_2, OWN)]
+    start(3, [(own_t, where, peer(1, m)) for m in range(7, 0, -1)], total.at[c, pl.ds(0, 7 * OWN)])
+    total[c, rows(off_2, OWN), :] = own_t[...]
     before = len(sent)
-    for s in streams:
-        started[3, s].wait_recv()
-        where = total.at[c, rows(off_1[s], PIECE[s])]
-        for part_at, masks in enumerate(((3, 2, 1), (7, 6, 5, 4))):
-            copies = [(where, where, peer(s, 0, m)) for m in masks]
-            start((4, s, part_at), copies, total.at[c, pl.ds(FIRST[s], len(masks) * PIECE[s])])
+    started[3].wait_recv()
+    where = total.at[c, rows(off_1, PIECE)]
+    for h, masks in enumerate(((3, 2, 1), (7, 6, 5, 4))):
+        start((4, h), [(where, where, peer(0, m)) for m in masks], total.at[c, pl.ds(0, len(masks) * PIECE)])
     drain(before)
-    for s in streams:
-        for part_at in range(2):
-            started[4, s, part_at].wait_recv()
-            begin = FIRST[s] + flip(z_low, part_at) * 4 * PIECE[s]
-            where = total.at[c, rows(begin, 4 * PIECE[s])]
-            start((5, s, part_at), [(where, where, other)], where)
-
-    def whole(half, s):
+    for h in range(2):
+        started[4, h].wait_recv()
+        where = total.at[c, rows(flip(z_low, h) * (ROWS // 2), ROWS // 2)]
+        start((5, h), [(where, where, other)], where)
+
+    def whole(half, late):
         for cc in range(CORES):
-            @pl.when(half == cc)
-            def _():
-                for kind, i, j, at in places(cc, k):
-                    if (at >= SIZES[0]) != s:
-                        continue
-                    if kind == "p":
-                        first[:, j * LANE : (j + 1) * LANE] = total[cc, at : at + k, :]
-                        continue
-                    v = total[cc, at : at + LANE, :]
-                    for a, e, w in ((i, j, v), (j, i, v.T))[: 2 if j > i else 1]:
-                        high, low = split(w)
-                        g_high[a * LANE : (a + 1) * LANE, e * LANE : (e + 1) * LANE] = high
-                        g_low[a * LANE : (a + 1) * LANE, e * LANE : (e + 1) * LANE] = low
-
-    for s in streams:
-        whole(c, s)
-    drain(len(sent) - 4)
-    for s in streams:
-        for part_at in range(2):
-            started[5, s, part_at].wait_recv()
-        whole(1 - c, s)
+            for h in range(2):
+                @pl.when((half == cc) & (late == h))
+                def _():
+                    for kind, i, j, at in places(cc, k):
+                        if (at >= ROWS // 2) != h:
+                            continue
+                        if kind == "p":
+                            first[:, j * LANE : (j + 1) * LANE] = total[cc, at : at + k, :]
+                            continue
+                        v = total[cc, at : at + LANE, :]
+                        for a, e, w in ((i, j, v), (j, i, v.T))[: 2 if j > i else 1]:
+                            high, low = split(w)
+                            g_high[a * LANE : (a + 1) * LANE, e * LANE : (e + 1) * LANE] = high
+                            g_low[a * LANE : (a + 1) * LANE, e * LANE : (e + 1) * LANE] = low
+
+    for h in range(2):
+        whole(c, jnp.int32(h))
+    drain(len(sent) - 2)
+    for h in range(2):
+        started[5, h].wait_recv()
+        whole(1 - c, flip(z_low, h))
     drain(len(sent))
 
 
@@ -346,7 +340,7 @@
     rows, d = slab.shape
     k = panel.shape[0]
     scale = math.sqrt(rows * nz * ny * nx * CORES)
-    n_sems = 2 * 16 + 2 * FAR - 1
+    n_sems = 2 * 9 + 2 * FAR - 1
     params = functools.partial(pltpu.CompilerParams, vmem_limit_bytes=36 * 1024 * 1024)
     vmem = pl.BlockSpec(memory_space=pltpu.VMEM)
 
@@ -358,13 +352,14 @@
         in_specs=[vmem] * 2,
         out_specs=(vmem,) * 3,
         scratch_shapes=[
-            pltpu.VMEM((CORES, HALF, LANE), F32),
-            pltpu.VMEM((HALF, LANE), F32),
-            *[pltpu.VMEM((7, size, LANE), F32) for size in PIECE + LAST],
+            pltpu.VMEM((CORES, ROWS, LANE), F32),
+            pltpu.VMEM((ROWS, LANE), F32),
+            pltpu.VMEM((7, PIECE, LANE), F32),
+            pltpu.VMEM((7, OWN, LANE), F32),
             pltpu.VMEM((OWN, LANE), F32),
             pltpu.VMEM((FAR, OWN, LANE), F32),
             pltpu.VMEM((OWN, LANE), F32),
-            pltpu.VMEM((CORES, HALF, LANE), F32),
+            pltpu.VMEM((CORES, ROWS, LANE), F32),
             pltpu.SemaphoreType.REGULAR((2,)),
             pltpu.SemaphoreType.DMA((n_sems,)),
         ],

time: 71.2 us -> 74 us (1.039)
  Pallas kernels: 68.3 us -> 71.1 us
    pallas_call x1, Pallas kernels: 58.3 us -> 61.1 us  [body(): pl.pallas_call(functools.partial(reduce_kernel, (nz, ny, nx)), out_shape=...]
where the time goes in v9:
time: 74 us; the launch traced here: 73.8 us
  Pallas kernels  71.1 us (96%)
  local copies, waits for them, and re-layouts  2.06 us (3%)
    pallas_call x1, Pallas kernels, body(): pl.pallas_call(functools.partial(reduce_kernel, (nz, ny, nx)), out_shape=...  61.1 us
    pallas_call x1, Pallas kernels, body(): pl.pallas_call(functools.partial(passes_kernel, scale), out_shape=(jax.Sh...  9.97 us
    unnamed x4, local copies, waits for them, and re-layouts  2.06 us

profile of v9, /device:TPU:1, one launch (start us, length us, event | category | flops | bytes accessed | tf_op | source)
XLA Modules:
  0.0 73.8 jit_solution(4047954106760484748)
XLA Ops:
  0.6 0.0 copy-start
  0.6 1.2 %copy-done = bf16[512,1024]{1,0:T(8,128)(2,1)S(1)} copy-done((bf16[512,1024]{1,0:T(8,128)(2,1)S(1)}, bf16[512,1024]{1,0:T(8,128)(2,1)}, u32[]{:S(2)}) %copy-start) | copy-done | bytes 1048600
  1.9 0.0 copy-start.1
  1.9 0.8 %copy-done.1 = bf16[64,512]{1,0:T(8,128)(2,1)S(1)} copy-done((bf16[64,512]{1,0:T(8,128)(2,1)S(1)}, bf16[64,512]{1,0:T(8,128)(2,1)}, u32[]{:S(2)}) %copy-start.1) | copy-done | bytes 65560
  2.7 61.1 %shard_map.41 = (bf16[1024,1024]{1,0:T(8,128)(2,1)S(1)}, bf16[1024,1024]{1,0:T(8,128)(2,1)S(1)}, f32[64,1024]{1,0:T(8,128)S(1)}) custom-call(bf16[512,1024]{1,0:T(8,128)(2,1)S(1)} %copy-done, bf16[64,512]{1,0:T(8,128)(2,1)S(1)} %copy-done.1), custom_call_target="tpu_custom_call" | custom-call | flops 1000000000 | bytes 10000000 | tf_op jit(solution)/shard_map/pallas_call | solution.py:347
  63.8 10.0 %shard_map.42 = (f32[64,512]{1,0:T(8,128)}, f32[64,64]{1,0:T(8,128)}) custom-call(bf16[512,1024]{1,0:T(8,128)(2,1)S(1)} %copy-done, bf16[1024,1024]{1,0:T(8,128)(2,1)S(1)} %get-tuple-element.5.g_high, bf16[1024,1024]{1,0:T(8,128)(2,1)S(1)} %get-tuple-element.6.g_low, f32[64,1024]{1,0:T(8,128)S(1)} %get-tuple-element.7.first), custom_call_target="tpu_custom_call" | custom-call | flops 2000000000 | bytes 3000000 | tf_op jit(solution)/shard_map/pallas_call | solution.py:369
Async XLA Ops:
  0.6 1.2 %copy-start = (bf16[512,1024]{1,0:T(8,128)(2,1)S(1)}, bf16[512,1024]{1,0:T(8,128)(2,1)}, u32[]{:S(2)}) copy-start(bf16[512,1024]{1,0:T(8,128)(2,1)} %slab.3) | copy-start | bytes 3145732
  1.9 0.8 %copy-start.1 = (bf16[64,512]{1,0:T(8,128)(2,1)S(1)}, bf16[64,512]{1,0:T(8,128)(2,1)}, u32[]{:S(2)}) copy-start(bf16[64,512]{1,0:T(8,128)(2,1)} %panel.1) | copy-start | bytes 196612

commit v10 on v8

--- a/solution.py
+++ b/solution.py
@@ -69,13 +69,14 @@
 
 
 JOBS = ((("g", 0, 8), ("g", 6, 8), ("p", 0, 4)), (("g", 2, 8), ("p", 4, 8), ("g", 4, 8)))
-EARLY = (1, 2)
-SIZES = (12 * LANE, 8 * LANE)
-FIRST = (0, SIZES[0])
+NEEDS = ((1, 1, 2, 3), (1, 2, 3, 3))
+SIZES = (8 * LANE, 4 * LANE, 4 * LANE, 4 * LANE)
+STREAMS = len(SIZES)
+FIRST = tuple(sum(SIZES[:s]) for s in range(STREAMS))
 HALF = sum(SIZES)
 PIECE = tuple(size // 8 for size in SIZES)
 LAST = tuple(size // 64 for size in SIZES)
-LAST_AT = (0, LAST[0])
+LAST_AT = tuple(first // 64 for first in FIRST)
 OWN = sum(LAST)
 FAR = 4
 
@@ -94,11 +95,11 @@
     return bit + mask - 2 * bit * mask
 
 
-def reduce_kernel(dims, slab, panel, g_high, g_low, first, part, got_c, got_1a, got_1b,
-                  got_2a, got_2b, own, got_z, own_t, total, known, sems):
+def reduce_kernel(dims, slab, panel, g_high, g_low, first, part, got_c, own, got_z, own_t,
+                  total, known, sems, *got):
     nz, ny, nx = dims
     k = panel.shape[0]
-    got_1, got_2 = (got_1a, got_1b), (got_2a, got_2b)
+    got_1, got_2 = got[:STREAMS], got[STREAMS:]
 
     z = lax.axis_index("rowa")
     b = lax.axis_index("rowb")
@@ -124,7 +125,7 @@
     def pick(pair, family):
         return tuple(a + family * (e - a) for a, e in zip(*pair))
 
-    families = [lax.rem(s + c, 2) for s in range(2)]
+    families = [lax.rem(s + c, 2) for s in range(STREAMS)]
     groups = [
         (
             [pick(pair, f) for pair in (pair_x, pair_y, pair_z)],
@@ -177,13 +178,13 @@
     def rows(off, count):
         return pl.ds(off if isinstance(off, int) else pl.multiple_of(off, 8), count)
 
-    def work(half, stream):
+    def work(half, s):
         for cc in range(CORES):
             @pl.when(half == cc)
             def _():
                 at = 0
                 for number, (kind, lo, hi) in enumerate(JOBS[cc]):
-                    mine = (number >= EARLY[cc]) == stream
+                    mine = (NEEDS[cc][s - 1] if s else 0) <= number < NEEDS[cc][s]
                     if mine and kind == "g":
                         v = dot(slab[:, lo * LANE : (lo + 2) * LANE].T, slab[:, lo * LANE : hi * LANE])
                     elif mine:
@@ -195,7 +196,7 @@
                                 part[cc, at : at + step, :] = v[i * step : (i + 1) * step, j * LANE : (j + 1) * LANE]
                             at += step
 
-    streams = range(2)
+    streams = range(STREAMS)
     off_1 = [FIRST[s] + index(s, 0, 0) * PIECE[s] for s in streams]
     off_2 = [off_1[s] + index(s, 1, 0) * LAST[s] for s in streams]
 
@@ -205,7 +206,7 @@
             pl.semaphore_wait(barrier, len(everyone))
         where = pl.ds(FIRST[s], SIZES[s])
         start(("c", s), [(part.at[1 - c, where], got_c.at[where], other)], got_c.at[where])
-    tell(0, [peer(s, 1, 4) for s in streams])
+    tell(0, [peer(s, 1, 4) for s in range(2)])
     for s in streams:
         work(c, s)
         started["c", s].wait_recv()
@@ -286,7 +287,7 @@
             @pl.when(half == cc)
             def _():
                 for kind, i, j, at in places(cc, k):
-                    if (at >= SIZES[0]) != s:
+                    if not FIRST[s] <= at < FIRST[s] + SIZES[s]:
                         continue
                     if kind == "p":
                         first[:, j * LANE : (j + 1) * LANE] = total[cc, at : at + k, :]
@@ -299,7 +300,7 @@
 
     for s in streams:
         whole(c, s)
-    drain(len(sent) - 4)
+    drain(len(sent) - 2 * STREAMS)
     for s in streams:
         for part_at in range(2):
             started[5, s, part_at].wait_recv()
@@ -346,7 +347,7 @@
     rows, d = slab.shape
     k = panel.shape[0]
     scale = math.sqrt(rows * nz * ny * nx * CORES)
-    n_sems = 2 * 16 + 2 * FAR - 1
+    n_sems = 2 * 8 * STREAMS + 2 * FAR - 1
     params = functools.partial(pltpu.CompilerParams, vmem_limit_bytes=36 * 1024 * 1024)
     vmem = pl.BlockSpec(memory_space=pltpu.VMEM)
 
@@ -360,13 +361,13 @@
         scratch_shapes=[
             pltpu.VMEM((CORES, HALF, LANE), F32),
             pltpu.VMEM((HALF, LANE), F32),
-            *[pltpu.VMEM((7, size, LANE), F32) for size in PIECE + LAST],
             pltpu.VMEM((OWN, LANE), F32),
             pltpu.VMEM((FAR, OWN, LANE), F32),
             pltpu.VMEM((OWN, LANE), F32),
             pltpu.VMEM((CORES, HALF, LANE), F32),
             pltpu.SemaphoreType.REGULAR((2,)),
             pltpu.SemaphoreType.DMA((n_sems,)),
+            *[pltpu.VMEM((7, size, LANE), F32) for size in PIECE + LAST],
         ],
         compiler_params=params(collective_id=0, has_side_effects=True),
         cost_estimate=pl.CostEstimate(flops=10**9, bytes_accessed=10**7, transcendentals=0),

time: 71.2 us -> 70 us (0.983)
  Pallas kernels: 68.3 us -> 67.1 us
    pallas_call x1, Pallas kernels: 58.3 us -> 57.1 us  [body(): pl.pallas_call(functools.partial(reduce_kernel, (nz, ny, nx)), out_shape=...]
where the time goes in v10:
time: 70 us; the launch traced here: 69.8 us
  Pallas kernels  67.1 us (96%)
  local copies, waits for them, and re-layouts  2.06 us (3%)
    pallas_call x1, Pallas kernels, body(): pl.pallas_call(functools.partial(reduce_kernel, (nz, ny, nx)), out_shape=...  57.1 us
    pallas_call x1, Pallas kernels, body(): pl.pallas_call(functools.partial(passes_kernel, scale), out_shape=(jax.Sh...  9.97 us
    unnamed x4, local copies, waits for them, and re-layouts  2.06 us

profile of v10, /device:TPU:1, one launch (start us, length us, event | category | flops | bytes accessed | tf_op | source)
XLA Modules:
  0.0 69.8 jit_solution(7241097577356840675)
XLA Ops:
  0.6 0.0 copy-start
  0.6 1.2 %copy-done = bf16[512,1024]{1,0:T(8,128)(2,1)S(1)} copy-done((bf16[512,1024]{1,0:T(8,128)(2,1)S(1)}, bf16[512,1024]{1,0:T(8,128)(2,1)}, u32[]{:S(2)}) %copy-start) | copy-done | bytes 1048600
  1.9 0.0 copy-start.1
  1.9 0.8 %copy-done.1 = bf16[64,512]{1,0:T(8,128)(2,1)S(1)} copy-done((bf16[64,512]{1,0:T(8,128)(2,1)S(1)}, bf16[64,512]{1,0:T(8,128)(2,1)}, u32[]{:S(2)}) %copy-start.1) | copy-done | bytes 65560
  2.7 57.1 %shard_map.41 = (bf16[1024,1024]{1,0:T(8,128)(2,1)S(1)}, bf16[1024,1024]{1,0:T(8,128)(2,1)S(1)}, f32[64,1024]{1,0:T(8,128)S(1)}) custom-call(bf16[512,1024]{1,0:T(8,128)(2,1)S(1)} %copy-done, bf16[64,512]{1,0:T(8,128)(2,1)S(1)} %copy-done.1), custom_call_target="tpu_custom_call" | custom-call | flops 1000000000 | bytes 10000000 | tf_op jit(solution)/shard_map/pallas_call | solution.py:354
  59.8 10.0 %shard_map.42 = (f32[64,512]{1,0:T(8,128)}, f32[64,64]{1,0:T(8,128)}) custom-call(bf16[512,1024]{1,0:T(8,128)(2,1)S(1)} %copy-done, bf16[1024,1024]{1,0:T(8,128)(2,1)S(1)} %get-tuple-element.5.g_high, bf16[1024,1024]{1,0:T(8,128)(2,1)S(1)} %get-tuple-element.6.g_low, f32[64,1024]{1,0:T(8,128)S(1)} %get-tuple-element.7.first), custom_call_target="tpu_custom_call" | custom-call | flops 2000000000 | bytes 3000000 | tf_op jit(solution)/shard_map/pallas_call | solution.py:375
Async XLA Ops:
  0.6 1.2 %copy-start = (bf16[512,1024]{1,0:T(8,128)(2,1)S(1)}, bf16[512,1024]{1,0:T(8,128)(2,1)}, u32[]{:S(2)}) copy-start(bf16[512,1024]{1,0:T(8,128)(2,1)} %slab.3) | copy-start | bytes 3145732
  1.9 0.8 %copy-start.1 = (bf16[64,512]{1,0:T(8,128)(2,1)S(1)}, bf16[64,512]{1,0:T(8,128)(2,1)}, u32[]{:S(2)}) copy-start(bf16[64,512]{1,0:T(8,128)(2,1)} %panel.1) | copy-start | bytes 196612

commit v11 on v10

--- a/solution.py
+++ b/solution.py
@@ -230,38 +230,39 @@
             for m in range(7, 0, -1)
         ]
         start((2, s), copies, got_2[s])
+    me_far = z // (nz // FAR)
+    far_at = used[0]
+    used[0] += STREAMS * (2 * FAR - 1)
+
+    def far_copy(s, q, slot):
+        mine, at = pl.ds(LAST_AT[s], LAST[s]), far_at + s * (2 * FAR - 1)
+        return pltpu.make_async_remote_copy(
+            src_ref=own.at[mine], dst_ref=got_z.at[slot, mine], send_sem=sems.at[at + q - 1],
+            recv_sem=sems.at[at + FAR - 1 + slot], device_id=far[q - 1], device_id_type=MESH,
+        )
+
+    before = len(sent)
+    pl.semaphore_wait(known.at[1], 2)
     for s in streams:
         started[2, s].wait_recv()
         v = got_c[rows(off_2[s], LAST[s]), :]
         for m in range(1, 8):
             v = v + got_2[s][m - 1]
         own[LAST_AT[s] : LAST_AT[s] + LAST[s], :] = v
-
-    me_far = z // (nz // FAR)
-    send_z, recv_z = used[0], used[0] + FAR - 1
-    used[0] += 2 * FAR - 1
-
-    def far_copy(q, slot):
-        return pltpu.make_async_remote_copy(
-            src_ref=own, dst_ref=got_z.at[slot], send_sem=sems.at[send_z + q - 1], recv_sem=sems.at[recv_z + slot],
-            device_id=far[q - 1], device_id_type=MESH,
-        )
-
-    pl.semaphore_wait(known.at[1], 2)
-    for q in (2, 1, 3):
-        far_copy(q, me_far).start()
-    got_z[me_far] = own[...]
-    drain(len(sent))
-    for q in range(1, FAR):
-        sent.append(far_copy(q, me_far))
-    for q in range(1, FAR):
-        far_copy(q, lax.rem(me_far + q, FAR)).wait_recv()
-    v = got_z[0]
-    for q in range(1, FAR):
-        v = v + got_z[q]
-    own_t[...] = v
-
-    for s in streams:
+        for q in (2, 1, 3):
+            far_copy(s, q, me_far).start()
+            sent.append(far_copy(s, q, me_far))
+        got_z[me_far, LAST_AT[s] : LAST_AT[s] + LAST[s], :] = v
+    drain(before)
+
+    for s in streams:
+        mine = slice(LAST_AT[s], LAST_AT[s] + LAST[s])
+        for q in range(1, FAR):
+            far_copy(s, q, lax.rem(me_far + q, FAR)).wait_recv()
+        v = got_z[0, mine, :]
+        for q in range(1, FAR):
+            v = v + got_z[q, mine, :]
+        own_t[mine, :] = v
         where = rows(off_2[s], LAST[s])
         src = own_t.at[pl.ds(LAST_AT[s], LAST[s])]
         copies = [(src, total.at[c, where], peer(s, 1, m)) for m in range(7, 0, -1)]
@@ -347,7 +348,7 @@
     rows, d = slab.shape
     k = panel.shape[0]
     scale = math.sqrt(rows * nz * ny * nx * CORES)
-    n_sems = 2 * 8 * STREAMS + 2 * FAR - 1
+    n_sems = STREAMS * (16 + 2 * FAR - 1)
     params = functools.partial(pltpu.CompilerParams, vmem_limit_bytes=36 * 1024 * 1024)
     vmem = pl.BlockSpec(memory_space=pltpu.VMEM)
 

time: 70 us -> 66.6 us (0.951)
  Pallas kernels: 67.1 us -> 63.6 us
    pallas_call x1, Pallas kernels: 57.1 us -> 53.7 us  [body(): pl.pallas_call(functools.partial(reduce_kernel, (nz, ny, nx)), out_shape=...]
where the time goes in v11:
time: 66.6 us; the launch traced here: 66.3 us
  Pallas kernels  63.6 us (95%)
  local copies, waits for them, and re-layouts  2.06 us (3%)
    pallas_call x1, Pallas kernels, body(): pl.pallas_call(functools.partial(reduce_kernel, (nz, ny, nx)), out_shape=...  53.7 us
    pallas_call x1, Pallas kernels, body(): pl.pallas_call(functools.partial(passes_kernel, scale), out_shape=(jax.Sh...  9.96 us
    unnamed x4, local copies, waits for them, and re-layouts  2.06 us

profile of v11, /device:TPU:1, one launch (start us, length us, event | category | flops | bytes accessed | tf_op | source)
XLA Modules:
  0.0 66.3 jit_solution(16809498676702755515)
XLA Ops:
  0.6 0.0 copy-start
  0.6 1.2 %copy-done = bf16[512,1024]{1,0:T(8,128)(2,1)S(1)} copy-done((bf16[512,1024]{1,0:T(8,128)(2,1)S(1)}, bf16[512,1024]{1,0:T(8,128)(2,1)}, u32[]{:S(2)}) %copy-start) | copy-done | bytes 1048600
  1.9 0.0 copy-start.1
  1.9 0.8 %copy-done.1 = bf16[64,512]{1,0:T(8,128)(2,1)S(1)} copy-done((bf16[64,512]{1,0:T(8,128)(2,1)S(1)}, bf16[64,512]{1,0:T(8,128)(2,1)}, u32[]{:S(2)}) %copy-start.1) | copy-done | bytes 65560
  2.7 53.7 %shard_map.41 = (bf16[1024,1024]{1,0:T(8,128)(2,1)S(1)}, bf16[1024,1024]{1,0:T(8,128)(2,1)S(1)}, f32[64,1024]{1,0:T(8,128)S(1)}) custom-call(bf16[512,1024]{1,0:T(8,128)(2,1)S(1)} %copy-done, bf16[64,512]{1,0:T(8,128)(2,1)S(1)} %copy-done.1), custom_call_target="tpu_custom_call" | custom-call | flops 1000000000 | bytes 10000000 | tf_op jit(solution)/shard_map/pallas_call | solution.py:355
  56.4 10.0 %shard_map.42 = (f32[64,512]{1,0:T(8,128)}, f32[64,64]{1,0:T(8,128)}) custom-call(bf16[512,1024]{1,0:T(8,128)(2,1)S(1)} %copy-done, bf16[1024,1024]{1,0:T(8,128)(2,1)S(1)} %get-tuple-element.5.g_high, bf16[1024,1024]{1,0:T(8,128)(2,1)S(1)} %get-tuple-element.6.g_low, f32[64,1024]{1,0:T(8,128)S(1)} %get-tuple-element.7.first), custom_call_target="tpu_custom_call" | custom-call | flops 2000000000 | bytes 3000000 | tf_op jit(solution)/shard_map/pallas_call | solution.py:376
Async XLA Ops:
  0.6 1.2 %copy-start = (bf16[512,1024]{1,0:T(8,128)(2,1)S(1)}, bf16[512,1024]{1,0:T(8,128)(2,1)}, u32[]{:S(2)}) copy-start(bf16[512,1024]{1,0:T(8,128)(2,1)} %slab.3) | copy-start | bytes 3145732
  1.9 0.8 %copy-start.1 = (bf16[64,512]{1,0:T(8,128)(2,1)S(1)}, bf16[64,512]{1,0:T(8,128)(2,1)}, u32[]{:S(2)}) copy-start(bf16[64,512]{1,0:T(8,128)(2,1)} %panel.1) | copy-start | bytes 196612

commit v12 on v11

--- a/solution.py
+++ b/solution.py
@@ -69,8 +69,8 @@
 
 
 JOBS = ((("g", 0, 8), ("g", 6, 8), ("p", 0, 4)), (("g", 2, 8), ("p", 4, 8), ("g", 4, 8)))
-NEEDS = ((1, 1, 2, 3), (1, 2, 3, 3))
-SIZES = (8 * LANE, 4 * LANE, 4 * LANE, 4 * LANE)
+NEEDS = ((1, 1, 1, 2, 3), (1, 1, 2, 3, 3))
+SIZES = (4 * LANE,) * 5
 STREAMS = len(SIZES)
 FIRST = tuple(sum(SIZES[:s]) for s in range(STREAMS))
 HALF = sum(SIZES)

time: 66.6 us -> 65.4 us (0.982)
  Pallas kernels: 63.6 us -> 62.5 us
    pallas_call x1, Pallas kernels: 53.7 us -> 52.5 us  [body(): pl.pallas_call(functools.partial(reduce_kernel, (nz, ny, nx)), out_shape=...]
where the time goes in v12:
time: 65.4 us; the launch traced here: 65.2 us
  Pallas kernels  62.5 us (96%)
  local copies, waits for them, and re-layouts  2.06 us (3%)
    pallas_call x1, Pallas kernels, body(): pl.pallas_call(functools.partial(reduce_kernel, (nz, ny, nx)), out_shape=...  52.5 us
    pallas_call x1, Pallas kernels, body(): pl.pallas_call(functools.partial(passes_kernel, scale), out_shape=(jax.Sh...  9.97 us
    unnamed x4, local copies, waits for them, and re-layouts  2.06 us

profile of v12, /device:TPU:1, one launch (start us, length us, event | category | flops | bytes accessed | tf_op | source)
XLA Modules:
  0.0 65.2 jit_solution(14675845004199560890)
XLA Ops:
  0.6 0.0 copy-start
  0.6 1.2 %copy-done = bf16[512,1024]{1,0:T(8,128)(2,1)S(1)} copy-done((bf16[512,1024]{1,0:T(8,128)(2,1)S(1)}, bf16[512,1024]{1,0:T(8,128)(2,1)}, u32[]{:S(2)}) %copy-start) | copy-done | bytes 1048600
  1.9 0.0 copy-start.1
  1.9 0.8 %copy-done.1 = bf16[64,512]{1,0:T(8,128)(2,1)S(1)} copy-done((bf16[64,512]{1,0:T(8,128)(2,1)S(1)}, bf16[64,512]{1,0:T(8,128)(2,1)}, u32[]{:S(2)}) %copy-start.1) | copy-done | bytes 65560
  2.7 52.5 %shard_map.41 = (bf16[1024,1024]{1,0:T(8,128)(2,1)S(1)}, bf16[1024,1024]{1,0:T(8,128)(2,1)S(1)}, f32[64,1024]{1,0:T(8,128)S(1)}) custom-call(bf16[512,1024]{1,0:T(8,128)(2,1)S(1)} %copy-done, bf16[64,512]{1,0:T(8,128)(2,1)S(1)} %copy-done.1), custom_call_target="tpu_custom_call" | custom-call | flops 1000000000 | bytes 10000000 | tf_op jit(solution)/shard_map/pallas_call | solution.py:355
  55.2 10.0 %shard_map.42 = (f32[64,512]{1,0:T(8,128)}, f32[64,64]{1,0:T(8,128)}) custom-call(bf16[512,1024]{1,0:T(8,128)(2,1)S(1)} %copy-done, bf16[1024,1024]{1,0:T(8,128)(2,1)S(1)} %get-tuple-element.5.g_high, bf16[1024,1024]{1,0:T(8,128)(2,1)S(1)} %get-tuple-element.6.g_low, f32[64,1024]{1,0:T(8,128)S(1)} %get-tuple-element.7.first), custom_call_target="tpu_custom_call" | custom-call | flops 2000000000 | bytes 3000000 | tf_op jit(solution)/shard_map/pallas_call | solution.py:376
Async XLA Ops:
  0.6 1.2 %copy-start = (bf16[512,1024]{1,0:T(8,128)(2,1)S(1)}, bf16[512,1024]{1,0:T(8,128)(2,1)}, u32[]{:S(2)}) copy-start(bf16[512,1024]{1,0:T(8,128)(2,1)} %slab.3) | copy-start | bytes 3145732
  1.9 0.8 %copy-start.1 = (bf16[64,512]{1,0:T(8,128)(2,1)S(1)}, bf16[64,512]{1,0:T(8,128)(2,1)}, u32[]{:S(2)}) copy-start(bf16[64,512]{1,0:T(8,128)(2,1)} %panel.1) | copy-start | bytes 196612
